TPU v7x, 32 devices: a whole 2x2x4 slice. The times are simulated.
32 devices in a mesh: lon: 8 (over z, x), lat: 4 (over y, core).
Axes of the slice: x: 2, y: 2, z: 4, core: 2. Of those that a mesh axis runs over, the one named last changes fastest.
Arguments:
- final_adjoint: float32 [4, 12, 128, 1024], P(None, None, 'lat', 'lon'), may hold values from -6 to 6
- drift_u: float32 [12, 128, 1024], P(None, 'lat', 'lon'), may hold values from -1 to 1
- drift_v: float32 [12, 128, 1024], P(None, 'lat', 'lon'), may hold values from -1 to 1
- wet_mask: int32 [12, 128, 1024], P(None, 'lat', 'lon'), may hold values 0 or 1
- bottom_level: int32 [128, 1024], P('lat', 'lon'), may hold values from 1 to 12
- viscosity: float32 [128, 1024], P('lat', 'lon'), may hold values from 0.004 to 0.02
- bulk_rate: float32 [4, 128, 1024], P(None, 'lat', 'lon'), may hold values from 0.05 to 0.3
- atmos_adjoint: float32 [3, 4, 128, 1024], P(None, None, 'lat', 'lon'), may hold values from -6 to 6
Outputs:
- start_adjoint: float32 [4, 12, 128, 1024], P(None, None, 'lat', 'lon')
- flux_adjoint: float32 [3, 4, 128, 1024], P(None, None, 'lat', 'lon')
All inputs are finite; a program needn't handle non-finite values. No bound on the sum of `wet_mask` on one device may be relied on, other than what follows from the above.
Results may differ from a plain program's by a relative error of at most 0.00002.
Values sent between devices are 32-bit elements; how exact they have to be, the bound alone decides.
A program may use at most 128 MiB of HBM per device.

v0:
```python
import math

import jax
import jax.numpy as jnp
from jax import lax
from jax.experimental import pallas as pl
from jax.experimental.pallas import tpu as pltpu
from jax.sharding import PartitionSpec as P

lap_weight = 0.04
mixing_rate = 0.15
drag_rate = 0.2
expansion = 0.2
contraction = 0.15
pressure_weight = 0.1
coriolis_scale = 0.2

MESH = pl.DeviceIdType.MESH
PAD = 8
BLOCK = 32


def roll_lanes(x, shift):
    shift = shift % x.shape[-1]
    return pltpu.roll(x, shift, x.ndim - 1) if shift else x


def east(x):
    return roll_lanes(x, -1)


def west(x):
    return roll_lanes(x, 1)


def north(x):
    return pltpu.roll(x, x.shape[0] - 1, 0)


def south(x):
    return pltpu.roll(x, 1, 0)


def make_kernel(n_lat, n_lon, fields, levels, rows, cols, window, q_share, q_pad):
    n = n_lat * n_lon
    wide = rows + 2 * PAD
    total_rows = rows * n_lat
    s_share = rows // n_lat
    lines = window * fields * s_share
    misc = 3 * levels
    groups = levels // 4

    def kernel(
        fa, du, dv, wm, bl, vi, br, at_hbm,
        out, flux,
        at, wi, bi,
        A0, A1, ST, S0, S1, SS, SC, ME, MW, RE, RW, F, FS, FE, FW, FRE, FRW,
        G, SB1, RB1, SB2, RB2,
        halo_send, halo_recv, f_send, f_recv, a2a_send, a2a_recv, in_sem,
    ):
        lat = lax.axis_index("lat")
        lon = lax.axis_index("lon")
        me = lat * n_lon + lon
        eastward = lax.rem(lon + 1, n_lon)
        westward = lax.rem(lon + n_lon - 1, n_lon)

        mid_rows = pl.ds(PAD, rows)
        loads = [
            pltpu.make_async_copy(src, dst, in_sem.at[i])
            for i, (src, dst) in enumerate([
                (at_hbm, at),
                (fa, A0.at[:, pl.ds(1, levels), mid_rows, :]),
                (du, ST.at[pl.ds(0, levels), mid_rows, :]),
                (dv, ST.at[pl.ds(levels, levels), mid_rows, :]),
                (wm, wi),
                (bl, bi),
                (vi, ST.at[misc, mid_rows, :]),
                (br, ST.at[pl.ds(misc + 2, fields), mid_rows, :]),
            ])
        ]
        for c in loads:
            c.start()

        barrier = pltpu.get_barrier_semaphore()

        @pl.loop(1, n)
        def _(k):
            other = lax.rem(me + k, n)
            pl.semaphore_signal(
                barrier, inc=1, device_id={"lat": other // n_lon, "lon": lax.rem(other, n_lon)},
                device_id_type=MESH,
            )

        lane = lax.broadcasted_iota(jnp.int32, (wide, cols), 1)
        place = lane & (BLOCK - 1)
        block = lane >> (BLOCK.bit_length() - 1)
        row = lax.broadcasted_iota(jnp.int32, (wide, cols), 0) + lat * rows - PAD
        inside = jnp.where((row >= 0) & (row < total_rows), 1.0, 0.0)
        own = slice(PAD, PAD + rows)
        low = slice(0, PAD)
        high = slice(PAD + rows, wide)

        def pack(planes):
            height = planes[0].shape[0]
            b = block[:height]
            x = roll_lanes(planes[0], -118)
            for f in range(1, 4):
                x = jnp.where(b == f, roll_lanes(planes[f], BLOCK * f - 118), x)
            return x

        def message(packed, base):
            height = packed[0].shape[0]
            p = place[:height] // 8
            x = roll_lanes(packed[0], -base)
            for j in range(1, len(packed)):
                x = jnp.where(p == j, roll_lanes(packed[j], 8 * j - base), x)
            return x

        def spread(packed, from_east, from_west, j):
            x = jnp.where(place < 10, packed, roll_lanes(packed, 12))
            x = jnp.where((place >= 10) & (place < 16), roll_lanes(from_east, 10 - 8 * j), x)
            return jnp.where((place >= 16) & (place < 22), roll_lanes(from_west, 14 - 8 * j), x)

        blank_levels = jnp.zeros((fields, 1, wide, cols), jnp.float32)
        for ref in (A0, A1):
            ref[:, 0:1] = blank_levels
            ref[:, levels + 1 : levels + 2] = blank_levels
        blank = jnp.zeros((wide, cols), jnp.float32)
        for ref in (S0, S1):
            ref[0] = blank
            ref[levels + 1] = blank

        def clear(part):
            A0[:, 1 : levels + 1, part, :] = jnp.zeros((fields, levels, PAD, cols), jnp.float32)
            ST[:, part, :] = jnp.zeros((misc + 2 + fields, PAD, cols), jnp.float32)
            F[:, part, :] = jnp.zeros((2 * fields, PAD, cols), jnp.float32)
            for ref in (RE, RW, FRE, FRW):
                ref[:, part, :] = jnp.zeros((ref.shape[0], PAD, cols), jnp.float32)

        @pl.when(lat == 0)
        def _():
            clear(low)

        @pl.when(lat == n_lat - 1)
        def _():
            clear(high)

        def statics_of(k, part):
            fourth = misc + k if k < 2 + fields else misc
            return [ST[k, part, :], ST[levels + k, part, :], ST[2 * levels + k, part, :], ST[fourth, part, :]]

        for c in loads[1:]:
            c.wait()
        for k in range(levels):
            ST[2 * levels + k, own, :] = wi[k].astype(jnp.float32)
        ST[misc + 1, own, :] = bi[...].astype(jnp.float32)

        for m in range(groups):
            packed = [pack([A0[f, 4 * m + j + 1, own, :] for f in range(4)]) for j in range(4)]
            ME[m] = message(packed, 2)
            MW[m] = message(packed, 10)
            packed = [pack(statics_of(4 * m + j, own)) for j in range(4)]
            ME[groups + m] = message(packed, 2)
            MW[groups + m] = message(packed, 10)

        def transposed(x):
            if x.shape[0] < cols:
                x = jnp.concatenate([x, jnp.zeros((cols - x.shape[0], cols), x.dtype)], axis=0)
            return x.T

        loads[0].wait()
        for b in range(n_lat):
            x = at[:, :, b * s_share : (b + 1) * s_share, :].reshape(lines, cols)
            t = transposed(x)
            for a in range(n_lon):
                at_row = (b * n_lon + a) * q_pad
                SB1[at_row : at_row + q_share, :] = t[a * q_share : (a + 1) * q_share]

        pl.semaphore_wait(barrier, n - 1)

        def remote(src, dst, send, recv, i, to_lat, to_lon):
            return pltpu.make_async_remote_copy(
                src_ref=src, dst_ref=dst, send_sem=send.at[i], recv_sem=recv.at[i],
                device_id={"lat": to_lat, "lon": to_lon}, device_id_type=MESH,
            )

        def strip_copies(to_e, to_w, from_e, from_w, send, recv, i):
            mid = pl.ds(PAD, rows)
            both = [
                remote(to_e, from_w.at[:, mid, :], send, recv, i, lat, eastward),
                remote(to_w, from_e.at[:, mid, :], send, recv, i + 1, lat, westward),
            ]
            top, bottom = pl.ds(rows - PAD, PAD), pl.ds(0, PAD)
            up = [
                remote(to_e.at[:, top, :], from_w.at[:, low, :], send, recv, i + 2, lat + 1, eastward),
                remote(to_w.at[:, top, :], from_e.at[:, low, :], send, recv, i + 3, lat + 1, westward),
            ]
            down = [
                remote(to_e.at[:, bottom, :], from_w.at[:, high, :], send, recv, i + 4, lat - 1, eastward),
                remote(to_w.at[:, bottom, :], from_e.at[:, high, :], send, recv, i + 5, lat - 1, westward),
            ]
            return both, up, down

        def start(copies):
            both, up, down = copies
            for c in both:
                c.start()

            @pl.when(lat < n_lat - 1)
            def _():
                for c in up:
                    c.start()

            @pl.when(lat > 0)
            def _():
                for c in down:
                    c.start()

        def finish_recv(copies):
            both, up, down = copies
            for c in both:
                c.wait_recv()

            @pl.when(lat > 0)
            def _():
                for c in up:
                    c.wait_recv()

            @pl.when(lat < n_lat - 1)
            def _():
                for c in down:
                    c.wait_recv()

        def finish_send(copies):
            both, up, down = copies
            for c in both:
                c.wait_send()

            @pl.when(lat < n_lat - 1)
            def _():
                for c in up:
                    c.wait_send()

            @pl.when(lat > 0)
            def _():
                for c in down:
                    c.wait_send()

        def place_of(device):
            return pl.ds(pl.multiple_of(device * q_pad, 8), q_pad)

        def exchange(src, dst, i):
            @pl.loop(1, n)
            def _(k):
                other = lax.rem(me + k, n)
                pltpu.make_async_remote_copy(
                    src_ref=src.at[place_of(other)], dst_ref=dst.at[place_of(me)],
                    send_sem=a2a_send.at[i], recv_sem=a2a_recv.at[i],
                    device_id={"lat": other // n_lon, "lon": lax.rem(other, n_lon)},
                    device_id_type=MESH,
                ).start()

            dst[place_of(me), :] = src[place_of(me), :]

        def all_of(src, dst, sem):
            some = pl.ds(0, (n - 1) * q_pad)
            return pltpu.make_async_copy(src.at[some], dst.at[some], sem)

        both, up, down = strip_copies(ME, MW, RE, RW, halo_send, halo_recv, 0)
        inner = pl.ds(1, levels)
        up = up + [
            remote(A0.at[:, inner, pl.ds(rows, PAD), :], A0.at[:, inner, low, :],
                   halo_send, halo_recv, 6, lat + 1, lon),
            remote(ST.at[:, pl.ds(rows, PAD), :], ST.at[:, low, :],
                   halo_send, halo_recv, 7, lat + 1, lon),
        ]
        down = down + [
            remote(A0.at[:, inner, pl.ds(PAD, PAD), :], A0.at[:, inner, high, :],
                   halo_send, halo_recv, 8, lat - 1, lon),
            remote(ST.at[:, pl.ds(PAD, PAD), :], ST.at[:, high, :],
                   halo_send, halo_recv, 9, lat - 1, lon),
        ]
        halo = (both, up, down)
        start(halo)
        exchange(SB1, RB1, 0)

        finish_recv(halo)
        everywhere = slice(0, wide)

        def replicate(x, g):
            x = jnp.where(block == g, x, 0.0)
            x = x + roll_lanes(x, 2 * BLOCK)
            return x + roll_lanes(x, BLOCK)

        rate = blank
        for k in range(levels):
            m, j = k // 4, k % 4
            S0[k + 1] = spread(pack([A0[f, k + 1] for f in range(4)]), RE[m], RW[m], j)
            x = spread(pack(statics_of(k, everywhere)), RE[groups + m], RW[groups + m], j)
            for g in range(3):
                SS[g * levels + k] = replicate(x, g)
            if k < 2:
                SC[k] = replicate(x, 3)
            elif k < 2 + fields:
                f = k - 2
                rate = jnp.where(block == f, roll_lanes(x, BLOCK * (f - 3)), rate)
        SC[2] = rate

        all_of(SB1, RB1, a2a_recv.at[0]).wait()
        for b in range(n_lat):
            parts = []
            for q in range(q_share):
                parts.append(RB1[pl.ds(b * n_lon * q_pad + q, n_lon, stride=q_pad), :])
            t = jnp.concatenate(parts, axis=0).T
            G[pl.ds(b, lines, stride=n_lat), :] = t[:lines]
        for i, step in ((0, 2), (1, 1)):
            for f in range(fields):
                at_row = (step * fields + f) * rows
                F[i * fields + f, own, :] = G[at_row : at_row + rows]
        packed = [pack([F[i * fields + f, own, :] for f in range(4)]) for i in range(2)]
        FE[0] = message(packed, 2)
        FW[0] = message(packed, 10)
        both, up, down = strip_copies(FE, FW, FRE, FRW, f_send, f_recv, 0)
        up = up + [remote(F.at[:, pl.ds(rows, PAD), :], F.at[:, low, :], f_send, f_recv, 6, lat + 1, lon)]
        down = down + [remote(F.at[:, pl.ds(PAD, PAD), :], F.at[:, high, :], f_send, f_recv, 7, lat - 1, lon)]
        f_halo = (both, up, down)
        start(f_halo)

        angle = math.pi * (row.astype(jnp.float32) + 0.5) / total_rows - math.pi / 2
        SC[3] = coriolis_scale * jnp.sin(angle)
        SC[4] = inside

        half_t = 0.5 * pressure_weight * expansion
        half_s = -0.5 * pressure_weight * contraction
        edge = (lane < 2) | (lane >= cols - 2)

        def laplace(x):
            return (east(x) + west(x)) + (north(x) + south(x)) - 4.0 * x

        def spatial(w, u, v, extra_u, extra_v, visc, mask):
            x = (lap_weight * w - laplace(visc * w)) * mask
            hw = 0.5 * w
            along, across = u * hw, v * hw
            if extra_u is not None:
                along, across = along + extra_u, across + extra_v
            return (
                (east(x + along) + west(x - along))
                + (north(x + across) + south(x - across))
                - 4.0 * x
            )

        def advance(A, S, B, R):
            def body(i, carry):
                cu, cv, cs = carry
                k = levels - 1 - i
                kf = k.astype(jnp.float32)
                lower = kf + jnp.where(k == 0, 1000.0, 0.0)
                mask, cor = SC[4], SC[3]

                depth = SC[1]
                visc = SC[0]
                wet = SS[2 * levels + k]
                up_wet = SS[2 * levels + jnp.where(k == 0, 0, k - 1)]
                down_wet = SS[2 * levels + jnp.where(k == levels - 1, k, k + 1)]
                a = S[k + 1]
                w = wet * a
                cs = cs + w
                c32, c64, c96 = roll_lanes(cs, 32), roll_lanes(cs, 64), roll_lanes(cs, 96)
                extra_u = jnp.where(block == 0, half_t * c64, jnp.where(block == 1, half_s * c96, 0.0))
                extra_v = jnp.where(block == 0, half_t * c32, jnp.where(block == 1, half_s * c64, 0.0))
                new = a + spatial(w, SS[k], SS[levels + k], extra_u, extra_v, visc, mask)
                new = new + jnp.where(depth > kf + 1.0, mixing_rate, 0.0) * (down_wet * S[k + 2] - w)
                new = new - jnp.where(depth > lower, mixing_rate, 0.0) * (w - up_wet * S[k])
                new = new - jnp.where((depth == kf + 1.0) & (block >= 2), drag_rate, 0.0) * w
                new = new + cor * jnp.where(
                    block == 3, roll_lanes(w, 32), jnp.where(block == 2, -roll_lanes(w, 96), 0.0)
                )
                R[k + 1] = new
                joined = jnp.where(place < 10, new, roll_lanes(new, -12))

                depth = ST[misc + 1]
                visc = ST[misc]
                wet = ST[2 * levels + k]
                up_wet = ST[2 * levels + jnp.where(k == 0, 0, k - 1)]
                down_wet = ST[2 * levels + jnp.where(k == levels - 1, k, k + 1)]
                mix_down = jnp.where(depth > kf + 1.0, mixing_rate, 0.0)
                mix_up = jnp.where(depth > lower, mixing_rate, 0.0)
                drag = jnp.where(depth == kf + 1.0, drag_rate, 0.0)
                wu = wet * A[2, k + 1]
                wv = wet * A[3, k + 1]
                cu = cu + wu
                cv = cv + wv
                for f in range(4):
                    a = A[f, k + 1]
                    w = (wet * a, wet * a, wu, wv)[f]
                    h = (half_t, half_s, 0.0, 0.0)[f]
                    eu = h * cu if f < 2 else None
                    ev = h * cv if f < 2 else None
                    new = a + spatial(w, ST[k], ST[levels + k], eu, ev, visc, mask)
                    new = new + mix_down * (down_wet * A[f, k + 2] - w)
                    new = new - mix_up * (w - up_wet * A[f, k])
                    if f == 2:
                        new = new - drag * w - cor * wv
                    if f == 3:
                        new = new - drag * w + cor * wu
                    B[f, k + 1] = jnp.where(edge, roll_lanes(joined, 118 - BLOCK * f), new)
                return cu, cv, cs

            lax.fori_loop(0, levels, body, (blank, blank, blank))

        wet_top = 2 * levels

        for f in range(fields):
            at_row = (2 * fields + f) * rows
            flux_rows = A0[f, 1, own, :] * ST[wet_top, own, :]
            G[at_row : at_row + rows] = flux_rows

        advance(A0, S0, A1, S1)
        finish_send(halo)
        finish_recv(f_halo)
        for i in range(2):
            x = pack([F[i * fields + f] for f in range(4)])
            FS[i] = spread(x, FRE[0], FRW[0], i)

        def surface(A, S, B, R, i):
            R[1] = R[1] + SS[wet_top] * SC[2] * (FS[i] - S[1])
            for f in range(fields):
                gain = ST[wet_top] * ST[misc + 2 + f]
                B[f, 1] = B[f, 1] + gain * (F[i * fields + f] - A[f, 1])

        def store_flux(A, step):
            for f in range(fields):
                at_row = (step * fields + f) * rows
                G[at_row : at_row + rows] = A[f, 1, own, :] * ST[wet_top, own, :]

        surface(A0, S0, A1, S1, 0)
        store_flux(A1, 1)
        advance(A1, S1, A0, S0)
        surface(A1, S1, A0, S0, 1)

        finish_send(f_halo)
        last = [G[f * rows : (f + 1) * rows] for f in range(fields)]
        for f in range(fields):
            F[f, own, :] = last[f]
        store_flux(A0, 0)
        for b in range(n_lat):
            t = transposed(G[pl.ds(b, lines, stride=n_lat), :])
            for q in range(q_share):
                SB2[pl.ds(b * n_lon * q_pad + q, n_lon, stride=q_pad), :] = t[q * n_lon : (q + 1) * n_lon]
        exchange(SB2, RB2, 1)

        advance(A0, S0, A1, S1)
        for f in range(fields):
            gain = ST[wet_top, own, :] * ST[misc + 2 + f, own, :]
            A1[f, 1, own, :] = A1[f, 1, own, :] + gain * (F[f, own, :] - A0[f, 1, own, :])
        out[...] = A1[:, 1 : levels + 1, own, :]

        all_of(SB2, RB2, a2a_recv.at[1]).wait()
        for b in range(n_lat):
            starts = [(b * n_lon + a) * q_pad for a in range(n_lon)]
            x = jnp.concatenate([RB2[i : i + q_share, :] for i in starts], axis=0)
            t = x.T[:lines]
            flux[:, :, b * s_share : (b + 1) * s_share, :] = t.reshape(window, fields, s_share, cols)
        all_of(SB1, RB1, a2a_send.at[0]).wait()
        all_of(SB2, RB2, a2a_send.at[1]).wait()

    return kernel


def local(
    final_adjoint, drift_u, drift_v, wet_mask, bottom_level, viscosity, bulk_rate, atmos_adjoint
):
    fields, levels, rows, cols = final_adjoint.shape
    window = atmos_adjoint.shape[0]
    n_lat, n_lon = lax.axis_size("lat"), lax.axis_size("lon")
    n = n_lat * n_lon
    wide = rows + 2 * PAD
    q_share = cols // n_lon
    q_pad = -(-q_share // 8) * 8
    groups = levels // 4

    def buf(*shape):
        return pltpu.VMEM(shape, jnp.float32)

    kernel = make_kernel(n_lat, n_lon, fields, levels, rows, cols, window, q_share, q_pad)
    f32 = jnp.float32
    anywhere = pl.BlockSpec(memory_space=pl.ANY)
    return pl.pallas_call(
        kernel,
        out_shape=(
            pltpu.VMEM(final_adjoint.shape, f32),
            pltpu.VMEM(atmos_adjoint.shape, f32),
        ),
        in_specs=[anywhere] * 8,
        out_specs=(pl.BlockSpec(memory_space=pltpu.VMEM),) * 2,
        scratch_shapes=[
            buf(window, fields, rows, cols),
            pltpu.VMEM((levels, rows, cols), jnp.int32), pltpu.VMEM((rows, cols), jnp.int32),
            buf(fields, levels + 2, wide, cols), buf(fields, levels + 2, wide, cols),
            buf(3 * levels + 2 + fields, wide, cols),
            buf(levels + 2, wide, cols), buf(levels + 2, wide, cols),
            buf(3 * levels, wide, cols), buf(5, wide, cols),
            buf(2 * groups, rows, cols), buf(2 * groups, rows, cols),
            buf(2 * groups, wide, cols), buf(2 * groups, wide, cols),
            buf(2 * fields, wide, cols), buf(2, wide, cols),
            buf(1, rows, cols), buf(1, rows, cols), buf(1, wide, cols), buf(1, wide, cols),
            buf(window * fields * rows, cols),
            buf(n * q_pad, cols), buf(n * q_pad, cols), buf(n * q_pad, cols), buf(n * q_pad, cols),
            pltpu.SemaphoreType.DMA((10,)), pltpu.SemaphoreType.DMA((10,)),
            pltpu.SemaphoreType.DMA((8,)), pltpu.SemaphoreType.DMA((8,)),
            pltpu.SemaphoreType.DMA((2,)), pltpu.SemaphoreType.DMA((2,)), pltpu.SemaphoreType.DMA((8,)),
        ],
        compiler_params=pltpu.CompilerParams(
            collective_id=0, has_side_effects=True, vmem_limit_bytes=60 * 1024 * 1024
        ),
    )(final_adjoint, drift_u, drift_v, wet_mask, bottom_level, viscosity, bulk_rate, atmos_adjoint)


def solution(mesh):
    in_specs = (
        P(None, None, "lat", "lon"),
        P(None, "lat", "lon"),
        P(None, "lat", "lon"),
        P(None, "lat", "lon"),
        P("lat", "lon"),
        P("lat", "lon"),
        P(None, "lat", "lon"),
        P(None, None, "lat", "lon"),
    )
    out_specs = (P(None, None, "lat", "lon"), P(None, None, "lat", "lon"))
    return jax.shard_map(local, mesh=mesh, in_specs=in_specs, out_specs=out_specs, check_vma=False)
```

profile of v0, /device:TPU:0, one launch (start us, length us, event | category | flops | bytes accessed | tf_op | source)
XLA Modules:
  0.0 44.2 jit_solution(13002226819253070800)
XLA Ops:
  0.6 42.0 %shard_map.95 = (f32[4,12,32,128]{3,2,1,0:T(8,128)S(1)}, f32[3,4,32,128]{3,2,1,0:T(8,128)S(1)}) custom-call(f32[4,12,32,128]{3,2,1,0:T(8,128)} %fa.1, f32[12,32,128]{2,1,0:T(8,128)} %du.1, f32[12,32,128]{2,1,0:T(8,128)} %dv.1, s32[12,32,128]{2,1,0:T(8,128)} %wm.1, s32[32,128]{1,0:T(8,128)} %bl.1, f32[32,128]{1,0:T(8,128)} %vi.1, f32[4,32,128]{2,1,0:T(8,128)} %br.1, ...), custom_call_target="tpu_custom_call" | custom-call | tf_op jit(solution)/shard_map/pallas_call | solution.py:488
  42.6 0.9 %copy.12 = f32[4,12,32,128]{3,2,1,0:T(8,128)} copy(f32[4,12,32,128]{3,2,1,0:T(8,128)S(1)} %get-tuple-element.2) | data formatting | bytes 1572864
  43.5 0.7 %copy.13 = f32[3,4,32,128]{3,2,1,0:T(8,128)} copy(f32[3,4,32,128]{3,2,1,0:T(8,128)S(1)} %get-tuple-element.3) | data formatting | bytes 393216
where the time goes:
time: 44.3 us; the launch traced here: 44.2 us
  Pallas kernels  42 us (95%)
  local copies, waits for them, and re-layouts  1.56 us (4%)
  between operations  0.64 us (1%)
    pallas_call x1, Pallas kernels, local(): pl.pallas_call(kernel, out_shape=(pltpu.VMEM(final_adjoint.shape, f32), p...  42 us
    unnamed x2, local copies, waits for them, and re-layouts  1.56 us

commit v1 on v0

v1 whole, which is shorter than its diff:
```python
import math

import jax
import jax.numpy as jnp
from jax import lax
from jax.experimental import pallas as pl
from jax.experimental.pallas import tpu as pltpu
from jax.sharding import PartitionSpec as P

lap_weight = 0.04
mixing_rate = 0.15
drag_rate = 0.2
expansion = 0.2
contraction = 0.15
pressure_weight = 0.1
coriolis_scale = 0.2

MESH = pl.DeviceIdType.MESH
PAD = 8
BLOCK = 32
UNROLL = 3


def roll_lanes(x, shift):
    shift = shift % x.shape[-1]
    return pltpu.roll(x, shift, x.ndim - 1) if shift else x


def east(x):
    return roll_lanes(x, -1)


def west(x):
    return roll_lanes(x, 1)


def north(x):
    return pltpu.roll(x, x.shape[0] - 1, 0)


def south(x):
    return pltpu.roll(x, 1, 0)


def make_kernel(n_lat, n_lon, fields, levels, rows, cols, window, q_share, q_pad):
    n = n_lat * n_lon
    wide = rows + 2 * PAD
    total_rows = rows * n_lat
    s_share = rows // n_lat
    lines = window * fields * s_share
    misc = 3 * levels
    groups = levels // 4
    strips = (fields + 3) * groups + 2
    messages = -(-strips // 4)

    def kernel(
        fa, du, dv, wm, bl, vi, br, at_hbm,
        out, flux,
        at, A0, A1, ST, WI, BI, SP, SN, SC, SG, J, ME, MW, RE, RW, F, FS, FE, FW, FRE, FRW,
        G, H, SB1, RB1, SB2, RB2,
        halo_send, halo_recv, side_send, side_recv, f_send, f_recv, a2a_send, a2a_recv, in_sem,
    ):
        lat = lax.axis_index("lat")
        lon = lax.axis_index("lon")
        me = lat * n_lon + lon
        eastward = lax.rem(lon + 1, n_lon)
        westward = lax.rem(lon + n_lon - 1, n_lon)

        mid_rows = pl.ds(PAD, rows)
        inner = pl.ds(1, levels)
        loads = [
            pltpu.make_async_copy(src, dst, in_sem.at[i])
            for i, (src, dst) in enumerate([
                (at_hbm, at),
                (fa, A0.at[:, inner, mid_rows, :]),
                (du, ST.at[pl.ds(0, levels), mid_rows, :]),
                (dv, ST.at[pl.ds(levels, levels), mid_rows, :]),
                (wm, WI.at[:, mid_rows, :]),
                (bl, BI.at[mid_rows, :]),
                (vi, ST.at[misc, mid_rows, :]),
                (br, ST.at[pl.ds(misc + 2, fields), mid_rows, :]),
            ])
        ]
        for c in loads:
            c.start()

        barrier = pltpu.get_barrier_semaphore()

        @pl.loop(1, n)
        def _(k):
            other = lax.rem(me + k, n)
            pl.semaphore_signal(
                barrier, inc=1, device_id={"lat": other // n_lon, "lon": lax.rem(other, n_lon)},
                device_id_type=MESH,
            )

        lane = lax.broadcasted_iota(jnp.int32, (wide, cols), 1)
        place = lane & (BLOCK - 1)
        block = lane >> (BLOCK.bit_length() - 1)
        row = lax.broadcasted_iota(jnp.int32, (wide, cols), 0) + lat * rows - PAD
        own = slice(PAD, PAD + rows)
        low = slice(0, PAD)
        high = slice(PAD + rows, wide)
        everything = slice(0, wide)

        def pack(planes):
            height = planes[0].shape[0]
            b = block[:height]
            x = roll_lanes(planes[0], -118)
            for f in range(1, 4):
                x = jnp.where(b == f, roll_lanes(planes[f], BLOCK * f - 118), x)
            return x

        def message(packed, base):
            height = packed[0].shape[0]
            p = place[:height] // 8
            x = roll_lanes(packed[0], -base)
            for j in range(1, len(packed)):
                x = jnp.where(p == j, roll_lanes(packed[j], 8 * j - base), x)
            return x

        def lay(packed):
            return jnp.where(place[: packed.shape[0]] < 10, packed, roll_lanes(packed, 12))

        for ref in (A0, A1):
            ref[:, 0:1] = jnp.zeros((fields, 1, wide, cols), jnp.float32)

        def clear(part):
            A0[:, 1 : levels + 1, part, :] = jnp.zeros((fields, levels, PAD, cols), jnp.float32)
            ST[:, part, :] = jnp.zeros((misc + 2 + fields, PAD, cols), jnp.float32)
            WI[:, part, :] = jnp.zeros((levels, PAD, cols), jnp.int32)
            BI[part, :] = jnp.zeros((PAD, cols), jnp.int32)
            F[:, part, :] = jnp.zeros((2 * fields, PAD, cols), jnp.float32)
            for ref in (RE, RW, FRE, FRW):
                ref[:, part, :] = jnp.zeros((ref.shape[0], PAD, cols), jnp.float32)

        @pl.when(lat == 0)
        def _():
            clear(low)

        @pl.when(lat == n_lat - 1)
        def _():
            clear(high)

        angle = math.pi * (row.astype(jnp.float32) + 0.5) / total_rows - math.pi / 2
        SC[2] = coriolis_scale * jnp.sin(angle)

        def remote(src, dst, send, recv, i, to_lat, to_lon):
            return pltpu.make_async_remote_copy(
                src_ref=src, dst_ref=dst, send_sem=send.at[i], recv_sem=recv.at[i],
                device_id={"lat": to_lat, "lon": to_lon}, device_id_type=MESH,
            )

        def strip_copies(to_e, to_w, from_e, from_w, send, recv):
            both = [
                remote(to_e, from_w.at[:, mid_rows, :], send, recv, 0, lat, eastward),
                remote(to_w, from_e.at[:, mid_rows, :], send, recv, 1, lat, westward),
            ]
            top, bottom = pl.ds(rows - PAD, PAD), pl.ds(0, PAD)
            up = [
                remote(to_e.at[:, top, :], from_w.at[:, low, :], send, recv, 2, lat + 1, eastward),
                remote(to_w.at[:, top, :], from_e.at[:, low, :], send, recv, 3, lat + 1, westward),
            ]
            down = [
                remote(to_e.at[:, bottom, :], from_w.at[:, high, :], send, recv, 4, lat - 1, eastward),
                remote(to_w.at[:, bottom, :], from_e.at[:, high, :], send, recv, 5, lat - 1, westward),
            ]
            return both, up, down

        def start(copies):
            both, up, down = copies
            for c in both:
                c.start()

            @pl.when(lat < n_lat - 1)
            def _():
                for c in up:
                    c.start()

            @pl.when(lat > 0)
            def _():
                for c in down:
                    c.start()

        def finish_recv(copies):
            both, up, down = copies
            for c in both:
                c.wait_recv()

            @pl.when(lat > 0)
            def _():
                for c in up:
                    c.wait_recv()

            @pl.when(lat < n_lat - 1)
            def _():
                for c in down:
                    c.wait_recv()

        def finish_send(copies):
            both, up, down = copies
            for c in both:
                c.wait_send()

            @pl.when(lat < n_lat - 1)
            def _():
                for c in up:
                    c.wait_send()

            @pl.when(lat > 0)
            def _():
                for c in down:
                    c.wait_send()

        def rims(to, start_row, i, to_lat):
            src, dst = pl.ds(start_row, PAD), to
            return [
                remote(fa.at[:, :, src, :], A0.at[:, inner, dst, :], halo_send, halo_recv, i, to_lat, lon),
                remote(du.at[:, src, :], ST.at[pl.ds(0, levels), dst, :], halo_send, halo_recv, i + 1, to_lat, lon),
                remote(dv.at[:, src, :], ST.at[pl.ds(levels, levels), dst, :], halo_send, halo_recv, i + 2, to_lat, lon),
                remote(wm.at[:, src, :], WI.at[:, dst, :], halo_send, halo_recv, i + 3, to_lat, lon),
                remote(bl.at[src, :], BI.at[dst, :], halo_send, halo_recv, i + 4, to_lat, lon),
                remote(vi.at[src, :], ST.at[misc, dst, :], halo_send, halo_recv, i + 5, to_lat, lon),
                remote(br.at[:, src, :], ST.at[pl.ds(misc + 2, fields), dst, :], halo_send, halo_recv, i + 6, to_lat, lon),
            ]

        halo = ([], rims(low, rows - PAD, 0, lat + 1), rims(high, 0, 7, lat - 1))
        side = strip_copies(ME, MW, RE, RW, side_send, side_recv)

        pl.semaphore_wait(barrier, n - 1)
        start(halo)

        def convert(part):
            for k in range(levels):
                ST[k, part, :] = 0.5 * ST[k, part, :]
                ST[levels + k, part, :] = 0.5 * ST[levels + k, part, :]
                ST[2 * levels + k, part, :] = WI[k, part, :].astype(jnp.float32)
            ST[misc + 1, part, :] = BI[part, :].astype(jnp.float32)

        def sources(i, part):
            if i < fields * groups:
                f, j = divmod(i, groups)
                return [A0[f, b * groups + j + 1, part, :] for b in range(4)]
            if i < (fields + 3) * groups:
                kind, j = divmod(i - fields * groups, groups)
                return [ST[kind * levels + b * groups + j, part, :] for b in range(4)]
            if i == (fields + 3) * groups:
                v, d = ST[misc, part, :], ST[misc + 1, part, :]
                return [v, d, v, d]
            return [ST[misc + 2 + f, part, :] for f in range(4)]

        for c in loads[1:]:
            c.wait()
        convert(own)
        for m in range(messages):
            ids = range(4 * m, min(4 * m + 4, strips))
            packed = [pack(sources(i, own)) for i in ids]
            ME[m] = message(packed, 4)
            MW[m] = message(packed, 10)
            for i, x in zip(ids, packed):
                SP[i, own, :] = lay(x)
        start(side)

        def transposed(x):
            if x.shape[0] < cols:
                x = jnp.concatenate([x, jnp.zeros((cols - x.shape[0], cols), x.dtype)], axis=0)
            return x.T

        loads[0].wait()
        for b in range(n_lat):
            x = at[:, :, b * s_share : (b + 1) * s_share, :].reshape(lines, cols)
            t = transposed(x)
            for a in range(n_lon):
                at_row = (b * n_lon + a) * q_pad
                SB1[at_row : at_row + q_share, :] = t[a * q_share : (a + 1) * q_share]

        def place_of(device):
            return pl.ds(pl.multiple_of(device * q_pad, 8), q_pad)

        def exchange(src, dst, i):
            @pl.loop(1, n)
            def _(k):
                other = lax.rem(me + k, n)
                pltpu.make_async_remote_copy(
                    src_ref=src.at[place_of(other)], dst_ref=dst.at[place_of(me)],
                    send_sem=a2a_send.at[i], recv_sem=a2a_recv.at[i],
                    device_id={"lat": other // n_lon, "lon": lax.rem(other, n_lon)},
                    device_id_type=MESH,
                ).start()

            dst[place_of(me), :] = src[place_of(me), :]

        def all_of(src, dst, sem):
            some = pl.ds(0, (n - 1) * q_pad)
            return pltpu.make_async_copy(src.at[some], dst.at[some], sem)

        exchange(SB1, RB1, 0)

        finish_recv(halo)
        for part in (low, high):
            convert(part)
            for i in range(strips):
                SP[i, part, :] = lay(pack(sources(i, part)))

        finish_recv(side)
        between = (place >= 10) & (place < 22)
        half = lane & 15
        for m in range(messages):
            from_e, from_w = RE[m], roll_lanes(RW[m], 6)
            even = jnp.where(half < 6, from_e, from_w)
            odd = jnp.where((half >= 8) & (half < 14), from_e, from_w)
            for p in range(min(4, strips - 4 * m)):
                x = roll_lanes((even, odd)[p % 2], 10 - 8 * p)
                SP[4 * m + p] = jnp.where(between, x, SP[4 * m + p])

        strip_u, strip_v, strip_wet = [(fields + i) * groups for i in range(3)]
        x = SP[(fields + 3) * groups]
        SC[0] = jnp.where((block & 1) == 0, x, roll_lanes(x, BLOCK))
        SC[1] = jnp.where((block & 1) == 1, x, roll_lanes(x, -BLOCK)) - (block * groups).astype(jnp.float32)
        x = SP[(fields + 3) * groups + 1]
        for f in range(fields):
            SG[f] = jnp.where(block == 0, SP[strip_wet] * roll_lanes(x, -BLOCK * f), 0.0)

        half_t = 0.5 * pressure_weight * expansion
        half_s = -0.5 * pressure_weight * contraction
        edge2 = (lane < 2) | (lane >= cols - 2)
        edge4 = (lane < 4) | (lane >= cols - 4)
        keep_low = jnp.where(lat > 0, 1.0, 0.0)
        keep_high = jnp.where(lat < n_lat - 1, 1.0, 0.0)

        def masked(x):
            return jnp.concatenate([x[low] * keep_low, x[own], x[high] * keep_high], axis=0)

        def spatial(w, u, v, extra_u, extra_v, visc, part):
            y = visc * w
            inner_lap = (north(y) + south(y)) - 4.0 * y
            z = lap_weight * w - masked(inner_lap)
            along, across = u * w, v * w
            if extra_u is not None:
                along, across = along + extra_u, across + extra_v
            vertical = north(z + across) + south(z - across)
            z, y, along = z[part], y[part], along[part]
            t = z - inner_lap[part]
            flat = (east(t + along) + west(t - along)) - (roll_lanes(y, -2) + roll_lanes(y, 2))
            return (flat + vertical[part]) - (4.0 * z + 2.0 * y)

        def strip_step(A, B):
            depth, visc, cor = SC[1], SC[0], SC[2]
            w = [[SP[strip_wet + j] * A[f * groups + j] for j in range(groups)] for f in range(fields)]
            sums = []
            for f in (2, 3):
                c = [w[f][groups - 1]]
                for j in range(groups - 2, -1, -1):
                    c.insert(0, c[0] + w[f][j])
                later = 0.0
                for b in range(1, 4):
                    later = later + jnp.where(block < 4 - b, roll_lanes(c[0], -BLOCK * b), 0.0)
                sums.append([x + later for x in c])
            down = []
            for j in range(groups):
                mix = jnp.where(depth > j + 1.0, mixing_rate, 0.0)
                down.append([
                    mix * ((w[f][j + 1] if j < groups - 1 else roll_lanes(w[f][0], -BLOCK)) - w[f][j])
                    for f in range(fields)
                ])
            for j in range(groups):
                drag = jnp.where(depth == j + 1.0, drag_rate, 0.0)
                u, v = SP[strip_u + j], SP[strip_v + j]
                for f in range(fields):
                    h = (half_t, half_s, 0.0, 0.0)[f]
                    eu = h * sums[0][j] if f < 2 else None
                    ev = h * sums[1][j] if f < 2 else None
                    x = w[f][j]
                    new = A[f * groups + j] + spatial(x, u, v, eu, ev, visc, everything)
                    up = down[j - 1][f] if j > 0 else roll_lanes(down[groups - 1][f], BLOCK)
                    new = new + (down[j][f] - up)
                    if f == 2:
                        new = new - (drag * x + cor * w[3][j])
                    if f == 3:
                        new = new - (drag * x - cor * w[2][j])
                    B[f * groups + j] = new
                    J[f * groups + j] = jnp.where(place < 10, new, roll_lanes(new, -12))

        wet_top = 2 * levels

        def begin(A):
            wet = ST[wet_top + levels - 1]
            w = [wet * A[f, levels] for f in range(fields)]
            nothing = jnp.zeros((wide, cols), jnp.float32)
            return (nothing, nothing, *w, nothing, nothing, nothing, nothing)

        def level(A, k, carry, part, write):
            cu, cv, *rest = carry
            w, g = rest[:4], rest[4:]
            kf = jnp.asarray(k, jnp.int32).astype(jnp.float32)
            first = kf + jnp.where(k == 0, 1000.0, 0.0)
            depth, visc, cor = ST[misc + 1], ST[misc], SC[2][part]
            wet_up = ST[wet_top + jnp.where(k == 0, 0, k - 1)]
            mix = jnp.where(depth > first, mixing_rate, 0.0)
            drag = jnp.where(depth[part] == kf + 1.0, drag_rate, 0.0)
            u, v = ST[k], ST[levels + k]
            cu, cv = cu + w[2], cv + w[3]
            w_up = [wet_up * A[f, k] for f in range(fields)]
            g_up = [mix * (w[f] - w_up[f]) for f in range(fields)]
            for f in range(fields):
                h = (half_t, half_s, 0.0, 0.0)[f]
                eu = h * cu if f < 2 else None
                ev = h * cv if f < 2 else None
                new = A[f, k + 1][part] + spatial(w[f], u, v, eu, ev, visc, part)
                new = new + (g[f][part] - g_up[f][part])
                if f == 2:
                    new = new - (drag * w[2][part] + cor * w[3][part])
                if f == 3:
                    new = new - (drag * w[3][part] - cor * w[2][part])
                write(f, k, new)
            return (cu, cv, *w_up, *g_up)

        def sweep(A, carry, first, last, part, write):
            def body(i, carry):
                for j in range(UNROLL):
                    carry = level(A, first - i * UNROLL - j, carry, part, write)
                return carry

            return lax.fori_loop(0, (first - last + 1) // UNROLL, body, carry)

        def fixed(f, k, part, edge, new):
            b = k // groups
            x = pltpu.roll(J[f * groups + lax.rem(k, groups), part, :], 118 - BLOCK * b, 1)
            return jnp.where(edge[part], x, new)

        def store_flux(A, step):
            for f in range(fields):
                at_row = (step * fields + f) * rows
                H[at_row : at_row + rows] = A[f, 1, own, :] * ST[wet_top, own, :]

        def surface(A, S, B, R, i):
            for f in range(fields):
                R[f * groups] = R[f * groups] + SG[f] * (FS[i * fields + f] - S[f * groups])
                gain = ST[wet_top] * ST[misc + 2 + f]
                B[f, 1] = B[f, 1] + gain * (F[i * fields + f] - A[f, 1])

        store_flux(A0, 2)
        strip_step(SP, SN)

        def write1(f, k, new):
            A1[f, k + 1] = fixed(f, k, everything, edge2, new)

        sweep(A0, begin(A0), levels - 1, 0, everything, write1)

        all_of(SB1, RB1, a2a_recv.at[0]).wait()
        for b in range(n_lat):
            parts = []
            for q in range(q_share):
                parts.append(RB1[pl.ds(b * n_lon * q_pad + q, n_lon, stride=q_pad), :])
            t = jnp.concatenate(parts, axis=0).T
            G[pl.ds(b, lines, stride=n_lat), :] = t[:lines]
        for i, step in ((0, 2), (1, 1)):
            for f in range(fields):
                at_row = (step * fields + f) * rows
                F[i * fields + f, own, :] = G[at_row : at_row + rows]
        packed = [pack([F[i * fields + f, own, :] for f in range(4)]) for i in range(2)]
        FE[0] = message(packed, 4)
        FW[0] = message(packed, 10)
        both, up, down = strip_copies(FE, FW, FRE, FRW, f_send, f_recv)
        up = up + [remote(F.at[:, pl.ds(rows, PAD), :], F.at[:, low, :], f_send, f_recv, 6, lat + 1, lon)]
        down = down + [remote(F.at[:, pl.ds(PAD, PAD), :], F.at[:, high, :], f_send, f_recv, 7, lat - 1, lon)]
        f_halo = (both, up, down)
        start(f_halo)

        def write2(f, k, new):
            A0[f, k + 1] = new

        carry = sweep(A1, begin(A1), levels - 1, groups, everything, write2)

        finish_recv(f_halo)
        for i in range(2):
            x = lay(pack([F[i * fields + f] for f in range(4)]))
            x = jnp.where((place >= 10) & (place < 16), roll_lanes(FRE[0], 10 - 8 * i), x)
            x = jnp.where((place >= 16) & (place < 22), roll_lanes(FRW[0], 16 - 8 * i), x)
            for f in range(fields):
                FS[i * fields + f] = roll_lanes(x, -BLOCK * f)
        surface(A0, SP, A1, SN, 0)
        store_flux(A1, 1)
        strip_step(SN, SP)
        sweep(A1, carry, groups - 1, 0, everything, write2)
        for f in range(fields):
            A0[f, 1] = fixed(f, 0, everything, edge2, A0[f, 1])
        surface(A1, SN, A0, SP, 1)
        store_flux(A0, 0)

        for b in range(n_lat):
            t = transposed(H[pl.ds(b, lines, stride=n_lat), :])
            for q in range(q_share):
                SB2[pl.ds(b * n_lon * q_pad + q, n_lon, stride=q_pad), :] = t[q * n_lon : (q + 1) * n_lon]
        exchange(SB2, RB2, 1)

        strip_step(SP, SN)

        def write3(f, k, new):
            out[f, k] = fixed(f, k, own, edge4, new)

        sweep(A0, begin(A0), levels - 1, 0, own, write3)
        for f in range(fields):
            gain = ST[wet_top, own, :] * ST[misc + 2 + f, own, :]
            out[f, 0] = out[f, 0] + gain * (G[f * rows : (f + 1) * rows] - A0[f, 1, own, :])

        all_of(SB2, RB2, a2a_recv.at[1]).wait()
        for b in range(n_lat):
            starts = [(b * n_lon + a) * q_pad for a in range(n_lon)]
            x = jnp.concatenate([RB2[i : i + q_share, :] for i in starts], axis=0)
            t = x.T[:lines]
            flux[:, :, b * s_share : (b + 1) * s_share, :] = t.reshape(window, fields, s_share, cols)
        finish_send(halo)
        finish_send(side)
        finish_send(f_halo)
        all_of(SB1, RB1, a2a_send.at[0]).wait()
        all_of(SB2, RB2, a2a_send.at[1]).wait()

    return kernel


def local(
    final_adjoint, drift_u, drift_v, wet_mask, bottom_level, viscosity, bulk_rate, atmos_adjoint
):
    fields, levels, rows, cols = final_adjoint.shape
    window = atmos_adjoint.shape[0]
    n_lat, n_lon = lax.axis_size("lat"), lax.axis_size("lon")
    n = n_lat * n_lon
    wide = rows + 2 * PAD
    q_share = cols // n_lon
    q_pad = -(-q_share // 8) * 8
    groups = levels // 4
    strips = (fields + 3) * groups + 2
    messages = -(-strips // 4)

    def buf(*shape):
        return pltpu.VMEM(shape, jnp.float32)

    kernel = make_kernel(n_lat, n_lon, fields, levels, rows, cols, window, q_share, q_pad)
    f32 = jnp.float32
    anywhere = pl.BlockSpec(memory_space=pl.ANY)
    return pl.pallas_call(
        kernel,
        out_shape=(
            pltpu.VMEM(final_adjoint.shape, f32),
            pltpu.VMEM(atmos_adjoint.shape, f32),
        ),
        in_specs=[anywhere] * 8,
        out_specs=(pl.BlockSpec(memory_space=pltpu.VMEM),) * 2,
        scratch_shapes=[
            buf(window, fields, rows, cols),
            buf(fields, levels + 1, wide, cols), buf(fields, levels + 1, wide, cols),
            buf(3 * levels + 2 + fields, wide, cols),
            pltpu.VMEM((levels, wide, cols), jnp.int32), pltpu.VMEM((wide, cols), jnp.int32),
            buf(strips, wide, cols), buf(fields * groups, wide, cols),
            buf(3, wide, cols), buf(fields, wide, cols), buf(fields * groups, wide, cols),
            buf(messages, rows, cols), buf(messages, rows, cols),
            buf(messages, wide, cols), buf(messages, wide, cols),
            buf(2 * fields, wide, cols), buf(2 * fields, wide, cols),
            buf(1, rows, cols), buf(1, rows, cols), buf(1, wide, cols), buf(1, wide, cols),
            buf(window * fields * rows, cols), buf(window * fields * rows, cols),
            buf(n * q_pad, cols), buf(n * q_pad, cols), buf(n * q_pad, cols), buf(n * q_pad, cols),
            pltpu.SemaphoreType.DMA((14,)), pltpu.SemaphoreType.DMA((14,)),
            pltpu.SemaphoreType.DMA((6,)), pltpu.SemaphoreType.DMA((6,)),
            pltpu.SemaphoreType.DMA((8,)), pltpu.SemaphoreType.DMA((8,)),
            pltpu.SemaphoreType.DMA((2,)), pltpu.SemaphoreType.DMA((2,)), pltpu.SemaphoreType.DMA((8,)),
        ],
        compiler_params=pltpu.CompilerParams(
            collective_id=0, has_side_effects=True, vmem_limit_bytes=60 * 1024 * 1024
        ),
    )(final_adjoint, drift_u, drift_v, wet_mask, bottom_level, viscosity, bulk_rate, atmos_adjoint)


def solution(mesh):
    in_specs = (
        P(None, None, "lat", "lon"),
        P(None, "lat", "lon"),
        P(None, "lat", "lon"),
        P(None, "lat", "lon"),
        P("lat", "lon"),
        P("lat", "lon"),
        P(None, "lat", "lon"),
        P(None, None, "lat", "lon"),
    )
    out_specs = (P(None, None, "lat", "lon"), P(None, None, "lat", "lon"))
    return jax.shard_map(local, mesh=mesh, in_specs=in_specs, out_specs=out_specs, check_vma=False)
```

time: 44.3 us -> 38 us (0.86)
  Pallas kernels: 42 us -> 35.6 us
    pallas_call x1, Pallas kernels: 42 us -> 35.6 us  [local(): pl.pallas_call(kernel, out_shape=(pltpu.VMEM(final_adjoint.shape, f32), p...]
where the time goes in v1:
time: 38 us; the launch traced here: 37.8 us
  Pallas kernels  35.6 us (94%)
  local copies, waits for them, and re-layouts  1.56 us (4%)
  between operations  0.64 us (2%)
    pallas_call x1, Pallas kernels, local(): pl.pallas_call(kernel, out_shape=(pltpu.VMEM(final_adjoint.shape, f32), p...  35.6 us
    unnamed x2, local copies, waits for them, and re-layouts  1.56 us

profile of v1, /device:TPU:0, one launch (start us, length us, event | category | flops | bytes accessed | tf_op | source)
XLA Modules:
  0.0 37.8 jit_solution(16257452078761512253)
XLA Ops:
  0.6 35.6 %shard_map.95 = (f32[4,12,32,128]{3,2,1,0:T(8,128)S(1)}, f32[3,4,32,128]{3,2,1,0:T(8,128)S(1)}) custom-call(f32[4,12,32,128]{3,2,1,0:T(8,128)} %fa.1, f32[12,32,128]{2,1,0:T(8,128)} %du.1, f32[12,32,128]{2,1,0:T(8,128)} %dv.1, s32[12,32,128]{2,1,0:T(8,128)} %wm.1, s32[32,128]{1,0:T(8,128)} %bl.1, f32[32,128]{1,0:T(8,128)} %vi.1, f32[4,32,128]{2,1,0:T(8,128)} %br.1, ...), custom_call_target="tpu_custom_call" | custom-call | tf_op jit(solution)/shard_map/pallas_call | solution.py:542
  36.3 0.9 %copy.12 = f32[4,12,32,128]{3,2,1,0:T(8,128)} copy(f32[4,12,32,128]{3,2,1,0:T(8,128)S(1)} %get-tuple-element.2) | data formatting | bytes 1572864
  37.2 0.7 %copy.13 = f32[3,4,32,128]{3,2,1,0:T(8,128)} copy(f32[3,4,32,128]{3,2,1,0:T(8,128)S(1)} %get-tuple-element.3) | data formatting | bytes 393216

commit v2 on v1

--- a/solution.py
+++ b/solution.py
@@ -42,12 +42,13 @@
     return pltpu.roll(x, 1, 0)
 
 
-def make_kernel(n_lat, n_lon, fields, levels, rows, cols, window, q_share, q_pad):
+def make_kernel(n_lat, n_lon, fields, levels, rows, cols, window, q_share):
     n = n_lat * n_lon
     wide = rows + 2 * PAD
     total_rows = rows * n_lat
     s_share = rows // n_lat
-    lines = window * fields * s_share
+    lines = fields * s_share
+    per = BLOCK // n_lon
     misc = 3 * levels
     groups = levels // 4
     strips = (fields + 3) * groups + 2
@@ -57,7 +58,7 @@
         fa, du, dv, wm, bl, vi, br, at_hbm,
         out, flux,
         at, A0, A1, ST, WI, BI, SP, SN, SC, SG, J, ME, MW, RE, RW, F, FS, FE, FW, FRE, FRW,
-        G, H, SB1, RB1, SB2, RB2,
+        Y, FL, SB, RB,
         halo_send, halo_recv, side_send, side_recv, f_send, f_recv, a2a_send, a2a_recv, in_sem,
     ):
         lat = lax.axis_index("lat")
@@ -261,40 +262,92 @@
                 SP[i, own, :] = lay(x)
         start(side)
 
-        def transposed(x):
-            if x.shape[0] < cols:
-                x = jnp.concatenate([x, jnp.zeros((cols - x.shape[0], cols), x.dtype)], axis=0)
-            return x.T
+        def across(x):
+            return jnp.concatenate([x] * 4, axis=0).T
+
+        def by_block(t, which):
+            height = t.shape[0] // 4
+            x = t[:height]
+            for r in range(1, 4):
+                x = jnp.where(which == r, t[r * height : (r + 1) * height], x)
+            return x
+
+        part_of = (lane[:lines] & (q_share - 1)) // per
+        part_block = block[:lines]
+
+        def pack_forcing(step, e, i):
+            for b in range(n_lat):
+                x = at[step, :, b * s_share : (b + 1) * s_share, :].reshape(lines, cols)
+                Y[b] = across(x)
+                for p in range(per):
+                    x = Y[b, pl.ds(p, n_lon, stride=q_share), :]
+                    for r in range(1, 4):
+                        x = jnp.where(block[:n_lon] == r, Y[b, pl.ds(per * r + p, n_lon, stride=q_share), :], x)
+                    SB[e, pl.ds(b * n_lon * 8 + i * per + p, n_lon, stride=8), :] = x
+
+        def unpack_forcing(e, i, to):
+            for b in range(n_lat):
+                x = jnp.concatenate(
+                    [RB[e, pl.ds(b * n_lon * 8 + i * per + p, n_lon, stride=8), :] for p in range(per)], axis=0
+                )
+                to[pl.ds(b, lines, stride=n_lat), :] = by_block(across(x), part_block)
+
+        def pack_flux(e, i):
+            for b in range(n_lat):
+                x = by_block(across(FL[pl.ds(b, lines, stride=n_lat), :]), block[:BLOCK])
+                for p in range(per):
+                    at_row = b * n_lon * 8 + i * per + p
+                    SB[e, pl.ds(at_row, n_lon, stride=8), :] = x[p * n_lon : (p + 1) * n_lon]
+
+        def unpack_flux(e, i, step):
+            for b in range(n_lat):
+                for p in range(per):
+                    x = RB[e, pl.ds(b * n_lon * 8 + i * per + p, n_lon, stride=8), :]
+                    for r in range(4):
+                        Y[b, pl.ds(per * r + p, n_lon, stride=q_share), :] = x
+                x = by_block(Y[b].T, part_of)
+                flux[step, :, b * s_share : (b + 1) * s_share, :] = x.reshape(fields, s_share, cols)
+
+        def place_of(device, size):
+            return pl.ds(pl.multiple_of(device * 8, 8), size)
+
+        def exchange(e, size):
+            def send(la, lo):
+                pltpu.make_async_remote_copy(
+                    src_ref=SB.at[e, place_of(la * n_lon + lo, size)], dst_ref=RB.at[e, place_of(me, size)],
+                    send_sem=a2a_send.at[e], recv_sem=a2a_recv.at[e],
+                    device_id={"lat": la, "lon": lo}, device_id_type=MESH,
+                ).start()
+
+            for dl in range(n_lat):
+                la = lax.rem(lat + dl, n_lat)
+                least = 1 if dl == 0 else 0
+                if n_lon <= 8:
+                    for dn in range(least, n_lon):
+                        send(la, lax.rem(lon + dn, n_lon))
+                else:
+                    @pl.loop(least, n_lon)
+                    def _(dn):
+                        send(la, lax.rem(lon + dn, n_lon))
+
+            RB[e, place_of(me, 8), :] = SB[e, place_of(me, 8), :]
+
+        def all_of(e, size, sem):
+            some = pl.ds(0, (n - 1) * size)
+            pltpu.make_async_copy(SB.at[e, some], RB.at[e, some], sem.at[e]).wait()
 
         loads[0].wait()
-        for b in range(n_lat):
-            x = at[:, :, b * s_share : (b + 1) * s_share, :].reshape(lines, cols)
-            t = transposed(x)
-            for a in range(n_lon):
-                at_row = (b * n_lon + a) * q_pad
-                SB1[at_row : at_row + q_share, :] = t[a * q_share : (a + 1) * q_share]
-
-        def place_of(device):
-            return pl.ds(pl.multiple_of(device * q_pad, 8), q_pad)
-
-        def exchange(src, dst, i):
-            @pl.loop(1, n)
-            def _(k):
-                other = lax.rem(me + k, n)
-                pltpu.make_async_remote_copy(
-                    src_ref=src.at[place_of(other)], dst_ref=dst.at[place_of(me)],
-                    send_sem=a2a_send.at[i], recv_sem=a2a_recv.at[i],
-                    device_id={"lat": other // n_lon, "lon": lax.rem(other, n_lon)},
-                    device_id_type=MESH,
-                ).start()
-
-            dst[place_of(me), :] = src[place_of(me), :]
-
-        def all_of(src, dst, sem):
-            some = pl.ds(0, (n - 1) * q_pad)
-            return pltpu.make_async_copy(src.at[some], dst.at[some], sem)
-
-        exchange(SB1, RB1, 0)
+        pack_forcing(2, 0, 0)
+        pack_forcing(1, 0, 1)
+        exchange(0, 2 * per)
+
+        def store_flux(A):
+            for f in range(fields):
+                FL[f * rows : (f + 1) * rows] = A[f, 1, own, :] * ST[2 * levels, own, :]
+
+        pack_forcing(0, 1, 0)
+        store_flux(A0)
+        pack_flux(1, 1)
 
         finish_recv(halo)
         for part in (low, high):
@@ -428,36 +481,17 @@
             x = pltpu.roll(J[f * groups + lax.rem(k, groups), part, :], 118 - BLOCK * b, 1)
             return jnp.where(edge[part], x, new)
 
-        def store_flux(A, step):
-            for f in range(fields):
-                at_row = (step * fields + f) * rows
-                H[at_row : at_row + rows] = A[f, 1, own, :] * ST[wet_top, own, :]
-
         def surface(A, S, B, R, i):
             for f in range(fields):
                 R[f * groups] = R[f * groups] + SG[f] * (FS[i * fields + f] - S[f * groups])
                 gain = ST[wet_top] * ST[misc + 2 + f]
                 B[f, 1] = B[f, 1] + gain * (F[i * fields + f] - A[f, 1])
 
-        store_flux(A0, 2)
-        strip_step(SP, SN)
-
-        def write1(f, k, new):
-            A1[f, k + 1] = fixed(f, k, everything, edge2, new)
-
-        sweep(A0, begin(A0), levels - 1, 0, everything, write1)
-
-        all_of(SB1, RB1, a2a_recv.at[0]).wait()
-        for b in range(n_lat):
-            parts = []
-            for q in range(q_share):
-                parts.append(RB1[pl.ds(b * n_lon * q_pad + q, n_lon, stride=q_pad), :])
-            t = jnp.concatenate(parts, axis=0).T
-            G[pl.ds(b, lines, stride=n_lat), :] = t[:lines]
-        for i, step in ((0, 2), (1, 1)):
+        all_of(0, 2 * per, a2a_recv)
+        for i in range(2):
+            unpack_forcing(0, i, FL)
             for f in range(fields):
-                at_row = (step * fields + f) * rows
-                F[i * fields + f, own, :] = G[at_row : at_row + rows]
+                F[i * fields + f, own, :] = FL[f * rows : (f + 1) * rows]
         packed = [pack([F[i * fields + f, own, :] for f in range(4)]) for i in range(2)]
         FE[0] = message(packed, 4)
         FW[0] = message(packed, 10)
@@ -466,6 +500,15 @@
         down = down + [remote(F.at[:, pl.ds(PAD, PAD), :], F.at[:, high, :], f_send, f_recv, 7, lat - 1, lon)]
         f_halo = (both, up, down)
         start(f_halo)
+        strip_step(SP, SN)
+
+        def write1(f, k, new):
+            A1[f, k + 1] = fixed(f, k, everything, edge2, new)
+
+        sweep(A0, begin(A0), levels - 1, 0, everything, write1)
+
+
+        exchange(1, 2 * per)
 
         def write2(f, k, new):
             A0[f, k + 1] = new
@@ -480,19 +523,17 @@
             for f in range(fields):
                 FS[i * fields + f] = roll_lanes(x, -BLOCK * f)
         surface(A0, SP, A1, SN, 0)
-        store_flux(A1, 1)
+        store_flux(A1)
+        pack_flux(2, 0)
+        exchange(2, per)
         strip_step(SN, SP)
         sweep(A1, carry, groups - 1, 0, everything, write2)
         for f in range(fields):
             A0[f, 1] = fixed(f, 0, everything, edge2, A0[f, 1])
         surface(A1, SN, A0, SP, 1)
-        store_flux(A0, 0)
-
-        for b in range(n_lat):
-            t = transposed(H[pl.ds(b, lines, stride=n_lat), :])
-            for q in range(q_share):
-                SB2[pl.ds(b * n_lon * q_pad + q, n_lon, stride=q_pad), :] = t[q * n_lon : (q + 1) * n_lon]
-        exchange(SB2, RB2, 1)
+        store_flux(A0)
+        pack_flux(3, 0)
+        exchange(3, per)
 
         strip_step(SP, SN)
 
@@ -500,21 +541,22 @@
             out[f, k] = fixed(f, k, own, edge4, new)
 
         sweep(A0, begin(A0), levels - 1, 0, own, write3)
+        all_of(1, 2 * per, a2a_recv)
+        unpack_forcing(1, 0, FL)
         for f in range(fields):
             gain = ST[wet_top, own, :] * ST[misc + 2 + f, own, :]
-            out[f, 0] = out[f, 0] + gain * (G[f * rows : (f + 1) * rows] - A0[f, 1, own, :])
-
-        all_of(SB2, RB2, a2a_recv.at[1]).wait()
-        for b in range(n_lat):
-            starts = [(b * n_lon + a) * q_pad for a in range(n_lon)]
-            x = jnp.concatenate([RB2[i : i + q_share, :] for i in starts], axis=0)
-            t = x.T[:lines]
-            flux[:, :, b * s_share : (b + 1) * s_share, :] = t.reshape(window, fields, s_share, cols)
+            out[f, 0] = out[f, 0] + gain * (FL[f * rows : (f + 1) * rows] - A0[f, 1, own, :])
+
+        unpack_flux(1, 1, 2)
+        all_of(2, per, a2a_recv)
+        unpack_flux(2, 0, 1)
+        all_of(3, per, a2a_recv)
+        unpack_flux(3, 0, 0)
         finish_send(halo)
         finish_send(side)
         finish_send(f_halo)
-        all_of(SB1, RB1, a2a_send.at[0]).wait()
-        all_of(SB2, RB2, a2a_send.at[1]).wait()
+        for e in range(4):
+            all_of(e, (2 * per, 2 * per, per, per)[e], a2a_send)
 
     return kernel
 
@@ -528,7 +570,6 @@
     n = n_lat * n_lon
     wide = rows + 2 * PAD
     q_share = cols // n_lon
-    q_pad = -(-q_share // 8) * 8
     groups = levels // 4
     strips = (fields + 3) * groups + 2
     messages = -(-strips // 4)
@@ -536,7 +577,7 @@
     def buf(*shape):
         return pltpu.VMEM(shape, jnp.float32)
 
-    kernel = make_kernel(n_lat, n_lon, fields, levels, rows, cols, window, q_share, q_pad)
+    kernel = make_kernel(n_lat, n_lon, fields, levels, rows, cols, window, q_share)
     f32 = jnp.float32
     anywhere = pl.BlockSpec(memory_space=pl.ANY)
     return pl.pallas_call(
@@ -558,12 +599,11 @@
             buf(messages, wide, cols), buf(messages, wide, cols),
             buf(2 * fields, wide, cols), buf(2 * fields, wide, cols),
             buf(1, rows, cols), buf(1, rows, cols), buf(1, wide, cols), buf(1, wide, cols),
-            buf(window * fields * rows, cols), buf(window * fields * rows, cols),
-            buf(n * q_pad, cols), buf(n * q_pad, cols), buf(n * q_pad, cols), buf(n * q_pad, cols),
+            buf(n_lat, cols, cols), buf(fields * rows, cols), buf(4, n * 8, cols), buf(4, n * 8, cols),
             pltpu.SemaphoreType.DMA((14,)), pltpu.SemaphoreType.DMA((14,)),
             pltpu.SemaphoreType.DMA((6,)), pltpu.SemaphoreType.DMA((6,)),
             pltpu.SemaphoreType.DMA((8,)), pltpu.SemaphoreType.DMA((8,)),
-            pltpu.SemaphoreType.DMA((2,)), pltpu.SemaphoreType.DMA((2,)), pltpu.SemaphoreType.DMA((8,)),
+            pltpu.SemaphoreType.DMA((4,)), pltpu.SemaphoreType.DMA((4,)), pltpu.SemaphoreType.DMA((8,)),
         ],
         compiler_params=pltpu.CompilerParams(
             collective_id=0, has_side_effects=True, vmem_limit_bytes=60 * 1024 * 1024

time: 38 us -> 32.7 us (0.86)
  Pallas kernels: 35.6 us -> 30.4 us
    pallas_call x1, Pallas kernels: 35.6 us -> 30.4 us  [local(): pl.pallas_call(kernel, out_shape=(pltpu.VMEM(final_adjoint.shape, f32), p...]
where the time goes in v2:
time: 32.7 us; the launch traced here: 32.6 us
  Pallas kernels  30.4 us (93%)
  local copies, waits for them, and re-layouts  1.56 us (5%)
  between operations  0.64 us (2%)
    pallas_call x1, Pallas kernels, local(): pl.pallas_call(kernel, out_shape=(pltpu.VMEM(final_adjoint.shape, f32), p...  30.4 us
    unnamed x2, local copies, waits for them, and re-layouts  1.56 us

profile of v2, /device:TPU:0, one launch (start us, length us, event | category | flops | bytes accessed | tf_op | source)
XLA Modules:
  0.0 32.6 jit_solution(5467456987802375659)
XLA Ops:
  0.6 30.4 %shard_map.95 = (f32[4,12,32,128]{3,2,1,0:T(8,128)S(1)}, f32[3,4,32,128]{3,2,1,0:T(8,128)S(1)}) custom-call(f32[4,12,32,128]{3,2,1,0:T(8,128)} %fa.1, f32[12,32,128]{2,1,0:T(8,128)} %du.1, f32[12,32,128]{2,1,0:T(8,128)} %dv.1, s32[12,32,128]{2,1,0:T(8,128)} %wm.1, s32[32,128]{1,0:T(8,128)} %bl.1, f32[32,128]{1,0:T(8,128)} %vi.1, f32[4,32,128]{2,1,0:T(8,128)} %br.1, ...), custom_call_target="tpu_custom_call" | custom-call | tf_op jit(solution)/shard_map/pallas_call | solution.py:583
  31.0 0.9 %copy.12 = f32[4,12,32,128]{3,2,1,0:T(8,128)} copy(f32[4,12,32,128]{3,2,1,0:T(8,128)S(1)} %get-tuple-element.2) | data formatting | bytes 1572864
  31.9 0.7 %copy.13 = f32[3,4,32,128]{3,2,1,0:T(8,128)} copy(f32[3,4,32,128]{3,2,1,0:T(8,128)S(1)} %get-tuple-element.3) | data formatting | bytes 393216

commit v3 on v2

--- a/solution.py
+++ b/solution.py
@@ -17,6 +17,7 @@
 
 MESH = pl.DeviceIdType.MESH
 PAD = 8
+RIM = 6
 BLOCK = 32
 UNROLL = 3
 
@@ -70,7 +71,7 @@
         mid_rows = pl.ds(PAD, rows)
         inner = pl.ds(1, levels)
         loads = [
-            pltpu.make_async_copy(src, dst, in_sem.at[i])
+            pltpu.make_async_copy(src, dst, in_sem.at[min(i, 2)])
             for i, (src, dst) in enumerate([
                 (at_hbm, at),
                 (fa, A0.at[:, inner, mid_rows, :]),
@@ -135,6 +136,16 @@
             for ref in (RE, RW, FRE, FRW):
                 ref[:, part, :] = jnp.zeros((ref.shape[0], PAD, cols), jnp.float32)
 
+        for part in (slice(0, PAD - RIM), slice(PAD + rows + RIM, wide)):
+            height = part.stop - part.start
+            A0[:, 1 : levels + 1, part, :] = jnp.zeros((fields, levels, height, cols), jnp.float32)
+            ST[:, part, :] = jnp.zeros((misc + 2 + fields, height, cols), jnp.float32)
+            WI[:, part, :] = jnp.zeros((levels, height, cols), jnp.int32)
+            BI[part, :] = jnp.zeros((height, cols), jnp.int32)
+            F[:, part, :] = jnp.zeros((2 * fields, height, cols), jnp.float32)
+            for ref in (RE, RW, FRE, FRW):
+                ref[:, part, :] = jnp.zeros((ref.shape[0], height, cols), jnp.float32)
+
         @pl.when(lat == 0)
         def _():
             clear(low)
@@ -152,84 +163,82 @@
                 device_id={"lat": to_lat, "lon": to_lon}, device_id_type=MESH,
             )
 
+        def filler(count):
+            height = max(h for h in range(1, wide + 1) if count % h == 0)
+            return ST.at[pl.ds(0, count // height), pl.ds(0, height)]
+
+        class Group:
+            def __init__(self, both, up, down, sends, recvs, counts):
+                self.copies, self.sends, self.recvs, self.counts = (both, up, down), sends, recvs, counts
+
+            def each(self, action, toward):
+                both, up, down = range(3)
+                if self.copies[both]:
+                    action(both)
+                pl.when(lat < n_lat - 1 if toward else lat > 0)(lambda: action(up))
+                pl.when(lat > 0 if toward else lat < n_lat - 1)(lambda: action(down))
+
+            def start(self):
+                def go(i):
+                    for c in self.copies[i]:
+                        c.start()
+
+                self.each(go, True)
+
+            def wait(self, sems, toward):
+                def done(i):
+                    some = filler(self.counts[i])
+                    pltpu.make_async_copy(some, some, sems.at[i]).wait()
+
+                self.each(done, toward)
+
+            def finish_recv(self):
+                self.wait(self.recvs, False)
+
+            def finish_send(self):
+                self.wait(self.sends, True)
+
+        low_rim, high_rim = pl.ds(PAD - RIM, RIM), pl.ds(PAD + rows, RIM)
+        top, bottom = pl.ds(rows - RIM, RIM), pl.ds(0, RIM)
+
         def strip_copies(to_e, to_w, from_e, from_w, send, recv):
             both = [
                 remote(to_e, from_w.at[:, mid_rows, :], send, recv, 0, lat, eastward),
-                remote(to_w, from_e.at[:, mid_rows, :], send, recv, 1, lat, westward),
+                remote(to_w, from_e.at[:, mid_rows, :], send, recv, 0, lat, westward),
             ]
-            top, bottom = pl.ds(rows - PAD, PAD), pl.ds(0, PAD)
             up = [
-                remote(to_e.at[:, top, :], from_w.at[:, low, :], send, recv, 2, lat + 1, eastward),
-                remote(to_w.at[:, top, :], from_e.at[:, low, :], send, recv, 3, lat + 1, westward),
+                remote(to_e.at[:, top, :], from_w.at[:, low_rim, :], send, recv, 1, lat + 1, eastward),
+                remote(to_w.at[:, top, :], from_e.at[:, low_rim, :], send, recv, 1, lat + 1, westward),
             ]
             down = [
-                remote(to_e.at[:, bottom, :], from_w.at[:, high, :], send, recv, 4, lat - 1, eastward),
-                remote(to_w.at[:, bottom, :], from_e.at[:, high, :], send, recv, 5, lat - 1, westward),
+                remote(to_e.at[:, bottom, :], from_w.at[:, high_rim, :], send, recv, 2, lat - 1, eastward),
+                remote(to_w.at[:, bottom, :], from_e.at[:, high_rim, :], send, recv, 2, lat - 1, westward),
             ]
             return both, up, down
 
-        def start(copies):
-            both, up, down = copies
-            for c in both:
-                c.start()
-
-            @pl.when(lat < n_lat - 1)
-            def _():
-                for c in up:
-                    c.start()
-
-            @pl.when(lat > 0)
-            def _():
-                for c in down:
-                    c.start()
-
-        def finish_recv(copies):
-            both, up, down = copies
-            for c in both:
-                c.wait_recv()
-
-            @pl.when(lat > 0)
-            def _():
-                for c in up:
-                    c.wait_recv()
-
-            @pl.when(lat < n_lat - 1)
-            def _():
-                for c in down:
-                    c.wait_recv()
-
-        def finish_send(copies):
-            both, up, down = copies
-            for c in both:
-                c.wait_send()
-
-            @pl.when(lat < n_lat - 1)
-            def _():
-                for c in up:
-                    c.wait_send()
-
-            @pl.when(lat > 0)
-            def _():
-                for c in down:
-                    c.wait_send()
-
-        def rims(to, start_row, i, to_lat):
-            src, dst = pl.ds(start_row, PAD), to
+        def rims(src, dst, i, to_lat):
             return [
                 remote(fa.at[:, :, src, :], A0.at[:, inner, dst, :], halo_send, halo_recv, i, to_lat, lon),
-                remote(du.at[:, src, :], ST.at[pl.ds(0, levels), dst, :], halo_send, halo_recv, i + 1, to_lat, lon),
-                remote(dv.at[:, src, :], ST.at[pl.ds(levels, levels), dst, :], halo_send, halo_recv, i + 2, to_lat, lon),
-                remote(wm.at[:, src, :], WI.at[:, dst, :], halo_send, halo_recv, i + 3, to_lat, lon),
-                remote(bl.at[src, :], BI.at[dst, :], halo_send, halo_recv, i + 4, to_lat, lon),
-                remote(vi.at[src, :], ST.at[misc, dst, :], halo_send, halo_recv, i + 5, to_lat, lon),
-                remote(br.at[:, src, :], ST.at[pl.ds(misc + 2, fields), dst, :], halo_send, halo_recv, i + 6, to_lat, lon),
+                remote(du.at[:, src, :], ST.at[pl.ds(0, levels), dst, :], halo_send, halo_recv, i, to_lat, lon),
+                remote(dv.at[:, src, :], ST.at[pl.ds(levels, levels), dst, :], halo_send, halo_recv, i, to_lat, lon),
+                remote(wm.at[:, src, :], WI.at[:, dst, :], halo_send, halo_recv, i, to_lat, lon),
+                remote(bl.at[src, :], BI.at[dst, :], halo_send, halo_recv, i, to_lat, lon),
+                remote(vi.at[src, :], ST.at[misc, dst, :], halo_send, halo_recv, i, to_lat, lon),
+                remote(br.at[:, src, :], ST.at[pl.ds(misc + 2, fields), dst, :], halo_send, halo_recv, i, to_lat, lon),
             ]
 
-        halo = ([], rims(low, rows - PAD, 0, lat + 1), rims(high, 0, 7, lat - 1))
-        side = strip_copies(ME, MW, RE, RW, side_send, side_recv)
+        planes = (fields + 3) * levels + 2 + fields
+        halo = Group(
+            [], rims(top, low_rim, 1, lat + 1), rims(bottom, high_rim, 2, lat - 1),
+            halo_send, halo_recv, (0, planes * RIM, planes * RIM),
+        )
+        side = Group(
+            *strip_copies(ME, MW, RE, RW, side_send, side_recv), side_send, side_recv,
+            (2 * messages * rows, 2 * messages * RIM, 2 * messages * RIM),
+        )
 
         pl.semaphore_wait(barrier, n - 1)
-        start(halo)
+        halo.start()
 
         def convert(part):
             for k in range(levels):
@@ -250,8 +259,9 @@
                 return [v, d, v, d]
             return [ST[misc + 2 + f, part, :] for f in range(4)]
 
-        for c in loads[1:]:
-            c.wait()
+        loads[1].wait()
+        some = filler((3 * levels + 2 + fields) * rows)
+        pltpu.make_async_copy(some, some, in_sem.at[2]).wait()
         convert(own)
         for m in range(messages):
             ids = range(4 * m, min(4 * m + 4, strips))
@@ -260,7 +270,7 @@
             MW[m] = message(packed, 10)
             for i, x in zip(ids, packed):
                 SP[i, own, :] = lay(x)
-        start(side)
+        side.start()
 
         def across(x):
             return jnp.concatenate([x] * 4, axis=0).T
@@ -349,13 +359,13 @@
         store_flux(A0)
         pack_flux(1, 1)
 
-        finish_recv(halo)
+        halo.finish_recv()
         for part in (low, high):
             convert(part)
             for i in range(strips):
                 SP[i, part, :] = lay(pack(sources(i, part)))
 
-        finish_recv(side)
+        side.finish_recv()
         between = (place >= 10) & (place < 22)
         half = lane & 15
         for m in range(messages):
@@ -496,10 +506,12 @@
         FE[0] = message(packed, 4)
         FW[0] = message(packed, 10)
         both, up, down = strip_copies(FE, FW, FRE, FRW, f_send, f_recv)
-        up = up + [remote(F.at[:, pl.ds(rows, PAD), :], F.at[:, low, :], f_send, f_recv, 6, lat + 1, lon)]
-        down = down + [remote(F.at[:, pl.ds(PAD, PAD), :], F.at[:, high, :], f_send, f_recv, 7, lat - 1, lon)]
-        f_halo = (both, up, down)
-        start(f_halo)
+        up = up + [remote(F.at[:, pl.ds(PAD + rows - RIM, RIM), :], F.at[:, low_rim, :], f_send, f_recv, 1, lat + 1, lon)]
+        down = down + [remote(F.at[:, pl.ds(PAD, RIM), :], F.at[:, high_rim, :], f_send, f_recv, 2, lat - 1, lon)]
+        f_halo = Group(
+            both, up, down, f_send, f_recv, (2 * rows, (2 + 2 * fields) * RIM, (2 + 2 * fields) * RIM),
+        )
+        f_halo.start()
         strip_step(SP, SN)
 
         def write1(f, k, new):
@@ -515,7 +527,7 @@
 
         carry = sweep(A1, begin(A1), levels - 1, groups, everything, write2)
 
-        finish_recv(f_halo)
+        f_halo.finish_recv()
         for i in range(2):
             x = lay(pack([F[i * fields + f] for f in range(4)]))
             x = jnp.where((place >= 10) & (place < 16), roll_lanes(FRE[0], 10 - 8 * i), x)
@@ -552,9 +564,9 @@
         unpack_flux(2, 0, 1)
         all_of(3, per, a2a_recv)
         unpack_flux(3, 0, 0)
-        finish_send(halo)
-        finish_send(side)
-        finish_send(f_halo)
+        halo.finish_send()
+        side.finish_send()
+        f_halo.finish_send()
         for e in range(4):
             all_of(e, (2 * per, 2 * per, per, per)[e], a2a_send)
 
@@ -600,10 +612,8 @@
             buf(2 * fields, wide, cols), buf(2 * fields, wide, cols),
             buf(1, rows, cols), buf(1, rows, cols), buf(1, wide, cols), buf(1, wide, cols),
             buf(n_lat, cols, cols), buf(fields * rows, cols), buf(4, n * 8, cols), buf(4, n * 8, cols),
-            pltpu.SemaphoreType.DMA((14,)), pltpu.SemaphoreType.DMA((14,)),
-            pltpu.SemaphoreType.DMA((6,)), pltpu.SemaphoreType.DMA((6,)),
-            pltpu.SemaphoreType.DMA((8,)), pltpu.SemaphoreType.DMA((8,)),
-            pltpu.SemaphoreType.DMA((4,)), pltpu.SemaphoreType.DMA((4,)), pltpu.SemaphoreType.DMA((8,)),
+            *[pltpu.SemaphoreType.DMA((3,))] * 6,
+            pltpu.SemaphoreType.DMA((4,)), pltpu.SemaphoreType.DMA((4,)), pltpu.SemaphoreType.DMA((3,)),
         ],
         compiler_params=pltpu.CompilerParams(
             collective_id=0, has_side_effects=True, vmem_limit_bytes=60 * 1024 * 1024

time: 32.7 us -> 31.9 us (0.976)
  Pallas kernels: 30.4 us -> 29.6 us
    pallas_call x1, Pallas kernels: 30.4 us -> 29.6 us  [local(): pl.pallas_call(kernel, out_shape=(pltpu.VMEM(final_adjoint.shape, f32), p...]
where the time goes in v3:
time: 31.9 us; the launch traced here: 31.8 us
  Pallas kernels  29.6 us (93%)
  local copies, waits for them, and re-layouts  1.56 us (5%)
  between operations  0.64 us (2%)
    pallas_call x1, Pallas kernels, local(): pl.pallas_call(kernel, out_shape=(pltpu.VMEM(final_adjoint.shape, f32), p...  29.6 us
    unnamed x2, local copies, waits for them, and re-layouts  1.56 us

profile of v3, /device:TPU:0, one launch (start us, length us, event | category | flops | bytes accessed | tf_op | source)
XLA Modules:
  0.0 31.8 jit_solution(1059108937278856211)
XLA Ops:
  0.6 29.6 %shard_map.95 = (f32[4,12,32,128]{3,2,1,0:T(8,128)S(1)}, f32[3,4,32,128]{3,2,1,0:T(8,128)S(1)}) custom-call(f32[4,12,32,128]{3,2,1,0:T(8,128)} %fa.1, f32[12,32,128]{2,1,0:T(8,128)} %du.1, f32[12,32,128]{2,1,0:T(8,128)} %dv.1, s32[12,32,128]{2,1,0:T(8,128)} %wm.1, s32[32,128]{1,0:T(8,128)} %bl.1, f32[32,128]{1,0:T(8,128)} %vi.1, f32[4,32,128]{2,1,0:T(8,128)} %br.1, ...), custom_call_target="tpu_custom_call" | custom-call | tf_op jit(solution)/shard_map/pallas_call | solution.py:595
  30.2 0.9 %copy.12 = f32[4,12,32,128]{3,2,1,0:T(8,128)} copy(f32[4,12,32,128]{3,2,1,0:T(8,128)S(1)} %get-tuple-element.2) | data formatting | bytes 1572864
  31.1 0.7 %copy.13 = f32[3,4,32,128]{3,2,1,0:T(8,128)} copy(f32[3,4,32,128]{3,2,1,0:T(8,128)S(1)} %get-tuple-element.3) | data formatting | bytes 393216

commit v4 on v3

--- a/solution.py
+++ b/solution.py
@@ -237,8 +237,83 @@
             (2 * messages * rows, 2 * messages * RIM, 2 * messages * RIM),
         )
 
-        pl.semaphore_wait(barrier, n - 1)
-        halo.start()
+        def across(x):
+            return jnp.concatenate([x] * 4, axis=0).T
+
+        def by_block(t, which):
+            height = t.shape[0] // 4
+            x = t[:height]
+            for r in range(1, 4):
+                x = jnp.where(which == r, t[r * height : (r + 1) * height], x)
+            return x
+
+        part_of = (lane[:lines] & (q_share - 1)) // per
+        part_block = block[:lines]
+
+        def pack_forcing(step, e, i):
+            for b in range(n_lat):
+                x = at[step, :, b * s_share : (b + 1) * s_share, :].reshape(lines, cols)
+                Y[b] = across(x)
+                for p in range(per):
+                    x = Y[b, pl.ds(p, n_lon, stride=q_share), :]
+                    for r in range(1, 4):
+                        x = jnp.where(block[:n_lon] == r, Y[b, pl.ds(per * r + p, n_lon, stride=q_share), :], x)
+                    SB[e, pl.ds(b * n_lon * 8 + i * per + p, n_lon, stride=8), :] = x
+
+        def unpack_forcing(e, i, to):
+            for b in range(n_lat):
+                x = jnp.concatenate(
+                    [RB[e, pl.ds(b * n_lon * 8 + i * per + p, n_lon, stride=8), :] for p in range(per)], axis=0
+                )
+                to[pl.ds(b, lines, stride=n_lat), :] = by_block(across(x), part_block)
+
+        def pack_flux(e, i):
+            for b in range(n_lat):
+                x = by_block(across(FL[pl.ds(b, lines, stride=n_lat), :]), block[:BLOCK])
+                for p in range(per):
+                    at_row = b * n_lon * 8 + i * per + p
+                    SB[e, pl.ds(at_row, n_lon, stride=8), :] = x[p * n_lon : (p + 1) * n_lon]
+
+        def unpack_flux(e, i, step):
+            for b in range(n_lat):
+                for p in range(per):
+                    x = RB[e, pl.ds(b * n_lon * 8 + i * per + p, n_lon, stride=8), :]
+                    for r in range(4):
+                        Y[b, pl.ds(per * r + p, n_lon, stride=q_share), :] = x
+                x = by_block(Y[b].T, part_of)
+                flux[step, :, b * s_share : (b + 1) * s_share, :] = x.reshape(fields, s_share, cols)
+
+        def place_of(device, size):
+            return pl.ds(pl.multiple_of(device * 8, 8), size)
+
+        def exchange(e, size):
+            def send(la, lo):
+                pltpu.make_async_remote_copy(
+                    src_ref=SB.at[e, place_of(la * n_lon + lo, size)], dst_ref=RB.at[e, place_of(me, size)],
+                    send_sem=a2a_send.at[e], recv_sem=a2a_recv.at[e],
+                    device_id={"lat": la, "lon": lo}, device_id_type=MESH,
+                ).start()
+
+            for dl in range(n_lat):
+                la = lax.rem(lat + dl, n_lat)
+                least = 1 if dl == 0 else 0
+                if n_lon <= 8:
+                    for dn in range(least, n_lon):
+                        send(la, lax.rem(lon + dn, n_lon))
+                else:
+                    @pl.loop(least, n_lon)
+                    def _(dn):
+                        send(la, lax.rem(lon + dn, n_lon))
+
+            RB[e, place_of(me, 8), :] = SB[e, place_of(me, 8), :]
+
+        def all_of(e, size, sem):
+            some = pl.ds(0, (n - 1) * size)
+            pltpu.make_async_copy(SB.at[e, some], RB.at[e, some], sem.at[e]).wait()
+
+        loads[0].wait()
+        pack_forcing(2, 0, 0)
+        pack_forcing(1, 0, 1)
 
         def convert(part):
             for k in range(levels):
@@ -270,86 +345,11 @@
             MW[m] = message(packed, 10)
             for i, x in zip(ids, packed):
                 SP[i, own, :] = lay(x)
+        pl.semaphore_wait(barrier, n - 1)
+        exchange(0, 2 * per)
+
         side.start()
-
-        def across(x):
-            return jnp.concatenate([x] * 4, axis=0).T
-
-        def by_block(t, which):
-            height = t.shape[0] // 4
-            x = t[:height]
-            for r in range(1, 4):
-                x = jnp.where(which == r, t[r * height : (r + 1) * height], x)
-            return x
-
-        part_of = (lane[:lines] & (q_share - 1)) // per
-        part_block = block[:lines]
-
-        def pack_forcing(step, e, i):
-            for b in range(n_lat):
-                x = at[step, :, b * s_share : (b + 1) * s_share, :].reshape(lines, cols)
-                Y[b] = across(x)
-                for p in range(per):
-                    x = Y[b, pl.ds(p, n_lon, stride=q_share), :]
-                    for r in range(1, 4):
-                        x = jnp.where(block[:n_lon] == r, Y[b, pl.ds(per * r + p, n_lon, stride=q_share), :], x)
-                    SB[e, pl.ds(b * n_lon * 8 + i * per + p, n_lon, stride=8), :] = x
-
-        def unpack_forcing(e, i, to):
-            for b in range(n_lat):
-                x = jnp.concatenate(
-                    [RB[e, pl.ds(b * n_lon * 8 + i * per + p, n_lon, stride=8), :] for p in range(per)], axis=0
-                )
-                to[pl.ds(b, lines, stride=n_lat), :] = by_block(across(x), part_block)
-
-        def pack_flux(e, i):
-            for b in range(n_lat):
-                x = by_block(across(FL[pl.ds(b, lines, stride=n_lat), :]), block[:BLOCK])
-                for p in range(per):
-                    at_row = b * n_lon * 8 + i * per + p
-                    SB[e, pl.ds(at_row, n_lon, stride=8), :] = x[p * n_lon : (p + 1) * n_lon]
-
-        def unpack_flux(e, i, step):
-            for b in range(n_lat):
-                for p in range(per):
-                    x = RB[e, pl.ds(b * n_lon * 8 + i * per + p, n_lon, stride=8), :]
-                    for r in range(4):
-                        Y[b, pl.ds(per * r + p, n_lon, stride=q_share), :] = x
-                x = by_block(Y[b].T, part_of)
-                flux[step, :, b * s_share : (b + 1) * s_share, :] = x.reshape(fields, s_share, cols)
-
-        def place_of(device, size):
-            return pl.ds(pl.multiple_of(device * 8, 8), size)
-
-        def exchange(e, size):
-            def send(la, lo):
-                pltpu.make_async_remote_copy(
-                    src_ref=SB.at[e, place_of(la * n_lon + lo, size)], dst_ref=RB.at[e, place_of(me, size)],
-                    send_sem=a2a_send.at[e], recv_sem=a2a_recv.at[e],
-                    device_id={"lat": la, "lon": lo}, device_id_type=MESH,
-                ).start()
-
-            for dl in range(n_lat):
-                la = lax.rem(lat + dl, n_lat)
-                least = 1 if dl == 0 else 0
-                if n_lon <= 8:
-                    for dn in range(least, n_lon):
-                        send(la, lax.rem(lon + dn, n_lon))
-                else:
-                    @pl.loop(least, n_lon)
-                    def _(dn):
-                        send(la, lax.rem(lon + dn, n_lon))
-
-            RB[e, place_of(me, 8), :] = SB[e, place_of(me, 8), :]
-
-        def all_of(e, size, sem):
-            some = pl.ds(0, (n - 1) * size)
-            pltpu.make_async_copy(SB.at[e, some], RB.at[e, some], sem.at[e]).wait()
-
-        loads[0].wait()
-        pack_forcing(2, 0, 0)
-        pack_forcing(1, 0, 1)
-        exchange(0, 2 * per)
+        halo.start()
 
         def store_flux(A):
             for f in range(fields):
@@ -512,6 +512,7 @@
             both, up, down, f_send, f_recv, (2 * rows, (2 + 2 * fields) * RIM, (2 + 2 * fields) * RIM),
         )
         f_halo.start()
+        exchange(1, 2 * per)
         strip_step(SP, SN)
 
         def write1(f, k, new):
@@ -519,8 +520,6 @@
 
         sweep(A0, begin(A0), levels - 1, 0, everything, write1)
 
-
-        exchange(1, 2 * per)
 
         def write2(f, k, new):
             A0[f, k + 1] = new

time: 31.9 us -> 30.2 us (0.947)
  Pallas kernels: 29.6 us -> 27.9 us
    pallas_call x1, Pallas kernels: 29.6 us -> 27.9 us  [local(): pl.pallas_call(kernel, out_shape=(pltpu.VMEM(final_adjoint.shape, f32), p...]
where the time goes in v4:
time: 30.2 us; the launch traced here: 30.1 us
  Pallas kernels  27.9 us (92%)
  local copies, waits for them, and re-layouts  1.56 us (5%)
  between operations  0.64 us (2%)
    pallas_call x1, Pallas kernels, local(): pl.pallas_call(kernel, out_shape=(pltpu.VMEM(final_adjoint.shape, f32), p...  27.9 us
    unnamed x2, local copies, waits for them, and re-layouts  1.56 us

profile of v4, /device:TPU:0, one launch (start us, length us, event | category | flops | bytes accessed | tf_op | source)
XLA Modules:
  0.0 30.1 jit_solution(9724843380817326867)
XLA Ops:
  0.6 27.9 %shard_map.95 = (f32[4,12,32,128]{3,2,1,0:T(8,128)S(1)}, f32[3,4,32,128]{3,2,1,0:T(8,128)S(1)}) custom-call(f32[4,12,32,128]{3,2,1,0:T(8,128)} %fa.1, f32[12,32,128]{2,1,0:T(8,128)} %du.1, f32[12,32,128]{2,1,0:T(8,128)} %dv.1, s32[12,32,128]{2,1,0:T(8,128)} %wm.1, s32[32,128]{1,0:T(8,128)} %bl.1, f32[32,128]{1,0:T(8,128)} %vi.1, f32[4,32,128]{2,1,0:T(8,128)} %br.1, ...), custom_call_target="tpu_custom_call" | custom-call | tf_op jit(solution)/shard_map/pallas_call | solution.py:594
  28.5 0.9 %copy.12 = f32[4,12,32,128]{3,2,1,0:T(8,128)} copy(f32[4,12,32,128]{3,2,1,0:T(8,128)S(1)} %get-tuple-element.2) | data formatting | bytes 1572864
  29.4 0.7 %copy.13 = f32[3,4,32,128]{3,2,1,0:T(8,128)} copy(f32[3,4,32,128]{3,2,1,0:T(8,128)S(1)} %get-tuple-element.3) | data formatting | bytes 393216

commit v5 on v4

--- a/solution.py
+++ b/solution.py
@@ -365,6 +365,21 @@
             for i in range(strips):
                 SP[i, part, :] = lay(pack(sources(i, part)))
 
+        all_of(0, 2 * per, a2a_recv)
+        for i in range(2):
+            unpack_forcing(0, i, FL)
+            for f in range(fields):
+                F[i * fields + f, own, :] = FL[f * rows : (f + 1) * rows]
+        packed = [pack([F[i * fields + f, own, :] for f in range(4)]) for i in range(2)]
+        FE[0] = message(packed, 4)
+        FW[0] = message(packed, 10)
+        both, up, down = strip_copies(FE, FW, FRE, FRW, f_send, f_recv)
+        up = up + [remote(F.at[:, pl.ds(PAD + rows - RIM, RIM), :], F.at[:, low_rim, :], f_send, f_recv, 1, lat + 1, lon)]
+        down = down + [remote(F.at[:, pl.ds(PAD, RIM), :], F.at[:, high_rim, :], f_send, f_recv, 2, lat - 1, lon)]
+        f_halo = Group(
+            both, up, down, f_send, f_recv, (2 * rows, (2 + 2 * fields) * RIM, (2 + 2 * fields) * RIM),
+        )
+        f_halo.start()
         side.finish_recv()
         between = (place >= 10) & (place < 22)
         half = lane & 15
@@ -497,21 +512,6 @@
                 gain = ST[wet_top] * ST[misc + 2 + f]
                 B[f, 1] = B[f, 1] + gain * (F[i * fields + f] - A[f, 1])
 
-        all_of(0, 2 * per, a2a_recv)
-        for i in range(2):
-            unpack_forcing(0, i, FL)
-            for f in range(fields):
-                F[i * fields + f, own, :] = FL[f * rows : (f + 1) * rows]
-        packed = [pack([F[i * fields + f, own, :] for f in range(4)]) for i in range(2)]
-        FE[0] = message(packed, 4)
-        FW[0] = message(packed, 10)
-        both, up, down = strip_copies(FE, FW, FRE, FRW, f_send, f_recv)
-        up = up + [remote(F.at[:, pl.ds(PAD + rows - RIM, RIM), :], F.at[:, low_rim, :], f_send, f_recv, 1, lat + 1, lon)]
-        down = down + [remote(F.at[:, pl.ds(PAD, RIM), :], F.at[:, high_rim, :], f_send, f_recv, 2, lat - 1, lon)]
-        f_halo = Group(
-            both, up, down, f_send, f_recv, (2 * rows, (2 + 2 * fields) * RIM, (2 + 2 * fields) * RIM),
-        )
-        f_halo.start()
         exchange(1, 2 * per)
         strip_step(SP, SN)
 

time: 30.2 us -> 30 us (level)
  no operation moved by 1% of the time
where the time goes in v5:
time: 30 us; the launch traced here: 29.8 us
  Pallas kernels  27.6 us (92%)
  local copies, waits for them, and re-layouts  1.56 us (5%)
  between operations  0.64 us (2%)
    pallas_call x1, Pallas kernels, local(): pl.pallas_call(kernel, out_shape=(pltpu.VMEM(final_adjoint.shape, f32), p...  27.6 us
    unnamed x2, local copies, waits for them, and re-layouts  1.56 us

profile of v5, /device:TPU:0, one launch (start us, length us, event | category | flops | bytes accessed | tf_op | source)
XLA Modules:
  0.0 29.8 jit_solution(17061526233259186339)
XLA Ops:
  0.6 27.6 %shard_map.95 = (f32[4,12,32,128]{3,2,1,0:T(8,128)S(1)}, f32[3,4,32,128]{3,2,1,0:T(8,128)S(1)}) custom-call(f32[4,12,32,128]{3,2,1,0:T(8,128)} %fa.1, f32[12,32,128]{2,1,0:T(8,128)} %du.1, f32[12,32,128]{2,1,0:T(8,128)} %dv.1, s32[12,32,128]{2,1,0:T(8,128)} %wm.1, s32[32,128]{1,0:T(8,128)} %bl.1, f32[32,128]{1,0:T(8,128)} %vi.1, f32[4,32,128]{2,1,0:T(8,128)} %br.1, ...), custom_call_target="tpu_custom_call" | custom-call | tf_op jit(solution)/shard_map/pallas_call | solution.py:594
  28.3 0.9 %copy.12 = f32[4,12,32,128]{3,2,1,0:T(8,128)} copy(f32[4,12,32,128]{3,2,1,0:T(8,128)S(1)} %get-tuple-element.2) | data formatting | bytes 1572864
  29.2 0.7 %copy.13 = f32[3,4,32,128]{3,2,1,0:T(8,128)} copy(f32[3,4,32,128]{3,2,1,0:T(8,128)S(1)} %get-tuple-element.3) | data formatting | bytes 393216

commit v6 on v5

--- a/solution.py
+++ b/solution.py
@@ -88,13 +88,19 @@
 
         barrier = pltpu.get_barrier_semaphore()
 
-        @pl.loop(1, n)
-        def _(k):
-            other = lax.rem(me + k, n)
-            pl.semaphore_signal(
-                barrier, inc=1, device_id={"lat": other // n_lon, "lon": lax.rem(other, n_lon)},
-                device_id_type=MESH,
-            )
+        def greet(la, lo):
+            pl.semaphore_signal(barrier, inc=1, device_id={"lat": la, "lon": lo}, device_id_type=MESH)
+
+        for dl in range(n_lat):
+            la = lax.rem(lat + dl, n_lat)
+            least = 1 if dl == 0 else 0
+            if n_lon <= 8:
+                for dn in range(least, n_lon):
+                    greet(la, lax.rem(lon + dn, n_lon))
+            else:
+                @pl.loop(least, n_lon)
+                def _(dn):
+                    greet(la, lax.rem(lon + dn, n_lon))
 
         lane = lax.broadcasted_iota(jnp.int32, (wide, cols), 1)
         place = lane & (BLOCK - 1)

time: 30 us -> 29.7 us (0.990)
  no operation moved by 1% of the time
where the time goes in v6:
time: 29.7 us; the launch traced here: 29.6 us
  Pallas kernels  27.4 us (92%)
  local copies, waits for them, and re-layouts  1.56 us (5%)
  between operations  0.64 us (2%)
    pallas_call x1, Pallas kernels, local(): pl.pallas_call(kernel, out_shape=(pltpu.VMEM(final_adjoint.shape, f32), p...  27.4 us
    unnamed x2, local copies, waits for them, and re-layouts  1.56 us

profile of v6, /device:TPU:0, one launch (start us, length us, event | category | flops | bytes accessed | tf_op | source)
XLA Modules:
  0.0 29.6 jit_solution(3460975651380658370)
XLA Ops:
  0.6 27.4 %shard_map.95 = (f32[4,12,32,128]{3,2,1,0:T(8,128)S(1)}, f32[3,4,32,128]{3,2,1,0:T(8,128)S(1)}) custom-call(f32[4,12,32,128]{3,2,1,0:T(8,128)} %fa.1, f32[12,32,128]{2,1,0:T(8,128)} %du.1, f32[12,32,128]{2,1,0:T(8,128)} %dv.1, s32[12,32,128]{2,1,0:T(8,128)} %wm.1, s32[32,128]{1,0:T(8,128)} %bl.1, f32[32,128]{1,0:T(8,128)} %vi.1, f32[4,32,128]{2,1,0:T(8,128)} %br.1, ...), custom_call_target="tpu_custom_call" | custom-call | tf_op jit(solution)/shard_map/pallas_call | solution.py:600
  28.0 0.9 %copy.12 = f32[4,12,32,128]{3,2,1,0:T(8,128)} copy(f32[4,12,32,128]{3,2,1,0:T(8,128)S(1)} %get-tuple-element.2) | data formatting | bytes 1572864
  28.9 0.7 %copy.13 = f32[3,4,32,128]{3,2,1,0:T(8,128)} copy(f32[3,4,32,128]{3,2,1,0:T(8,128)S(1)} %get-tuple-element.3) | data formatting | bytes 393216
